TPU v7x, 32 devices: a whole 2x2x4 slice. The times are simulated.
32 devices in a mesh: dp: 16 (over z, y, core), fsdp: 2 (over x).
Axes of the slice: x: 2, y: 2, z: 4, core: 2. Of those that a mesh axis runs over, the one named last changes fastest.
Arguments:
- tokens: bfloat16 [32, 2, 128, 1024], P(('dp', 'fsdp')), may hold values from -6 to 6
- encoded: bfloat16 [32, 512, 1024], P(('dp', 'fsdp')), may hold values from -6 to 6
- cotangent: bfloat16 [32, 2, 128, 1024], P(('dp', 'fsdp')), may hold values from -12 to 12
- buckets: int32 [32, 2, 128, 256], P(('dp', 'fsdp')), may hold values from 0 to 31
- lengths: int32 [32], P(('dp', 'fsdp')), may hold values from 32 to 128, as said below
- self_q: bfloat16 [1024, 1024], P(('dp', 'fsdp')), may hold values from -0.1875 to 0.1875
- self_qb: bfloat16 [1024], P(('dp', 'fsdp')), may hold values from -1.75 to 1.75
- self_k: bfloat16 [1024, 1024], P(('dp', 'fsdp')), may hold values from -0.1875 to 0.1875
- self_v: bfloat16 [1024, 1024], P(('dp', 'fsdp')), may hold values from -0.1875 to 0.1875
- self_vb: bfloat16 [1024], P(('dp', 'fsdp')), may hold values from -1.75 to 1.75
- self_o: bfloat16 [1024, 1024], P(('dp', 'fsdp')), may hold values from -0.75 to 0.75
- self_ob: bfloat16 [1024], P(('dp', 'fsdp')), may hold values from -1.75 to 1.75
- bucket_w: bfloat16 [1024, 512], P(('dp', 'fsdp')), may hold values from -0.1875 to 0.1875
- bucket_b: bfloat16 [512], P(('dp', 'fsdp')), may hold values from -3 to 3
- cross_q: bfloat16 [1024, 1024], P(('dp', 'fsdp')), may hold values from -0.1875 to 0.1875
- cross_qb: bfloat16 [1024], P(('dp', 'fsdp')), may hold values from -1.75 to 1.75
- cross_k: bfloat16 [1024, 1024], P(('dp', 'fsdp')), may hold values from -0.1875 to 0.1875
- cross_v: bfloat16 [1024, 1024], P(('dp', 'fsdp')), may hold values from -0.1875 to 0.1875
- cross_vb: bfloat16 [1024], P(('dp', 'fsdp')), may hold values from -1.75 to 1.75
- cross_o: bfloat16 [1024, 1024], P(('dp', 'fsdp')), may hold values from -1 to 1
- cross_ob: bfloat16 [1024], P(('dp', 'fsdp')), may hold values from -1.75 to 1.75
- ffn_in: bfloat16 [1024, 4096], P(('dp', 'fsdp')), may hold values from -0.1875 to 0.1875
- ffn_inb: bfloat16 [4096], P(('dp', 'fsdp')), may hold values from -1.75 to 1.75
- ffn_out: bfloat16 [4096, 1024], P(('dp', 'fsdp')), may hold values from -0.125 to 0.125
- ffn_outb: bfloat16 [1024], P(('dp', 'fsdp')), may hold values from -1.75 to 1.75
- gain_a: bfloat16 [1024], P(('dp', 'fsdp')), may hold values from 0.5 to 1.5
- shift_a: bfloat16 [1024], P(('dp', 'fsdp')), may hold values from -1.75 to 1.75
- gain_b: bfloat16 [1024], P(('dp', 'fsdp')), may hold values from 0.5 to 1.5
- shift_b: bfloat16 [1024], P(('dp', 'fsdp')), may hold values from -1.75 to 1.75
- gain_c: bfloat16 [1024], P(('dp', 'fsdp')), may hold values from 0.5 to 1.5
- shift_c: bfloat16 [1024], P(('dp', 'fsdp')), may hold values from -1.75 to 1.75
Outputs:
- outputs: bfloat16 [32, 2, 128, 1024], P(('dp', 'fsdp'))
- grad_tokens: float32 [32, 2, 128, 1024], P(('dp', 'fsdp'))
- grad_encoded: float32 [32, 512, 1024], P(('dp', 'fsdp'))
- grad_self_q: float32 [1024, 1024], P(('dp', 'fsdp'))
- grad_self_qb: float32 [1024], P(('dp', 'fsdp'))
- grad_self_k: float32 [1024, 1024], P(('dp', 'fsdp'))
- grad_self_v: float32 [1024, 1024], P(('dp', 'fsdp'))
- grad_self_vb: float32 [1024], P(('dp', 'fsdp'))
- grad_self_o: float32 [1024, 1024], P(('dp', 'fsdp'))
- grad_self_ob: float32 [1024], P(('dp', 'fsdp'))
- grad_bucket_w: float32 [1024, 512], P(('dp', 'fsdp'))
- grad_bucket_b: float32 [512], P(('dp', 'fsdp'))
- grad_cross_q: float32 [1024, 1024], P(('dp', 'fsdp'))
- grad_cross_qb: float32 [1024], P(('dp', 'fsdp'))
- grad_cross_k: float32 [1024, 1024], P(('dp', 'fsdp'))
- grad_cross_v: float32 [1024, 1024], P(('dp', 'fsdp'))
- grad_cross_vb: float32 [1024], P(('dp', 'fsdp'))
- grad_cross_o: float32 [1024, 1024], P(('dp', 'fsdp'))
- grad_cross_ob: float32 [1024], P(('dp', 'fsdp'))
- grad_ffn_in: float32 [1024, 4096], P(('dp', 'fsdp'))
- grad_ffn_inb: float32 [4096], P(('dp', 'fsdp'))
- grad_ffn_out: float32 [4096, 1024], P(('dp', 'fsdp'))
- grad_ffn_outb: float32 [1024], P(('dp', 'fsdp'))
- grad_gain_a: float32 [1024], P(('dp', 'fsdp'))
- grad_shift_a: float32 [1024], P(('dp', 'fsdp'))
- grad_gain_b: float32 [1024], P(('dp', 'fsdp'))
- grad_shift_b: float32 [1024], P(('dp', 'fsdp'))
- grad_gain_c: float32 [1024], P(('dp', 'fsdp'))
- grad_shift_c: float32 [1024], P(('dp', 'fsdp'))
Inputs may be any that keep to these rules, and one draw needn't show every extreme that they name: Target lengths; some item has 128 and some item has 32.
All inputs are finite; a program needn't handle non-finite values.
Results may differ from a plain program's by a relative error of at most 0.023.
Values may be sent and summed in bfloat16 or wider, within the bound.
A program may use at most 320 MiB of HBM per device.

v0:
```python
from functools import partial

import jax
import jax.numpy as jnp
from jax import lax
from jax.sharding import PartitionSpec as P

HEAD_DIM = 64
BUCKETS = 32


def product(left, right):
    return jnp.dot(left, right, preferred_element_type=jnp.float32)


def product_left(left, right):
    return lax.dot_general(
        left, right, (((0,), (0,)), ((), ())), preferred_element_type=jnp.float32
    )


def product_right(left, right):
    return lax.dot_general(
        left, right, (((1,), (1,)), ((), ())), preferred_element_type=jnp.float32
    )


def column_sum(grad):
    return jnp.sum(grad.astype(jnp.float32), axis=0)


def layer_norm(summed, gain, shift):
    center = summed - jnp.mean(summed, axis=-1, keepdims=True)
    spread = jnp.mean(center * center, axis=-1, keepdims=True)
    return center * lax.rsqrt(spread + 1e-05) * gain.astype(jnp.float32) + shift.astype(jnp.float32)


def norm_back(summed, gain, shift, grad):
    unused, pull = jax.vjp(layer_norm, summed, gain.astype(jnp.float32), shift.astype(jnp.float32))
    return pull(grad)


def visible(target):
    place = jnp.arange(2 * target, dtype=jnp.int32) % target
    stream = jnp.arange(2 * target, dtype=jnp.int32) // target
    row_place = place[:, None]
    key_place = place[None, :]
    row_stream = stream[:, None]
    key_stream = stream[None, :]
    earlier = (key_stream == 0) & (
        (row_stream == 0) & (key_place <= row_place) | (row_stream == 1) & (key_place < row_place)
    )
    itself = (key_stream == 1) & (row_stream == 1) & (key_place == row_place)
    return earlier | itself


def valid_rows(lengths, target):
    valid = (jnp.arange(target, dtype=jnp.int32)[None, :] < lengths[:, None]).astype(jnp.float32)
    return jnp.concatenate([valid, valid], axis=1).reshape(-1)


def bucket_table(buckets):
    count, streams, target, width = buckets.shape
    flat = buckets.reshape(count, streams * target, width)
    return (
        flat[:, :, None, :] == jnp.arange(BUCKETS, dtype=jnp.int32)[None, None, :, None]
    ).astype(jnp.float32)


def relative_bias(onehot, relative):
    table = relative.reshape(onehot.shape[0], onehot.shape[1], -1, BUCKETS)
    return jnp.einsum("nqbk,nqhb->nhqk", onehot, table, precision=lax.Precision.HIGHEST)


def scores_of(query, keys, bias, allowed):
    scores = (
        jnp.einsum("nqhd,nkhd->nhqk", query, keys, preferred_element_type=jnp.float32) * 0.125
        + bias
    )
    return jnp.where(allowed, scores, -1e30)


def attend(query, keys, values, bias, allowed):
    scores = scores_of(query, keys, bias, allowed)
    top = jnp.max(scores, axis=-1, keepdims=True)
    logsum = top + jnp.log(jnp.sum(jnp.exp(scores - top), axis=-1, keepdims=True))
    probs = jnp.exp(scores - logsum).astype(jnp.bfloat16)
    mixed = jnp.einsum("nhqk,nkhd->nqhd", probs, values, preferred_element_type=jnp.float32)
    return (mixed.astype(jnp.bfloat16), logsum)


def attend_back(query, keys, values, bias, allowed, logsum, grad_out):
    probs = jnp.exp(scores_of(query, keys, bias, allowed) - logsum)
    grad_probs = jnp.einsum("nqhd,nkhd->nhqk", grad_out, values, preferred_element_type=jnp.float32)
    grad_scores = (
        probs * (grad_probs - jnp.sum(probs * grad_probs, axis=-1, keepdims=True))
    ).astype(jnp.bfloat16)
    grad_query = (
        jnp.einsum("nhqk,nkhd->nqhd", grad_scores, keys, preferred_element_type=jnp.float32) * 0.125
    ).astype(jnp.bfloat16)
    grad_keys = (
        jnp.einsum("nhqk,nqhd->nkhd", grad_scores, query, preferred_element_type=jnp.float32)
        * 0.125
    ).astype(jnp.bfloat16)
    grad_values = jnp.einsum(
        "nhqk,nqhd->nkhd", probs.astype(jnp.bfloat16), grad_out, preferred_element_type=jnp.float32
    ).astype(jnp.bfloat16)
    return (grad_scores, grad_query, grad_keys, grad_values)


def forward(whole, tokens, encoded, buckets):
    (
        self_q,
        self_qb,
        self_k,
        self_v,
        self_vb,
        self_o,
        self_ob,
        bucket_w,
        bucket_b,
        cross_q,
        cross_qb,
        cross_k,
        cross_v,
        cross_vb,
        cross_o,
        cross_ob,
        ffn_in,
        ffn_inb,
        ffn_out,
        ffn_outb,
        gain_a,
        shift_a,
        gain_b,
        shift_b,
        gain_c,
        shift_c,
    ) = whole
    count, streams, target, width = tokens.shape
    source = encoded.shape[1]
    head_shape = (count, streams * target, width // HEAD_DIM, HEAD_DIM)
    source_shape = (count, source, width // HEAD_DIM, HEAD_DIM)
    rows = tokens.reshape(-1, width)
    enc_rows = encoded.reshape(-1, width)
    allowed = visible(target)
    query = (product(rows, self_q) + self_qb).astype(jnp.bfloat16)
    keys = product(rows, self_k).astype(jnp.bfloat16)
    values = (product(rows, self_v) + self_vb).astype(jnp.bfloat16)
    relative = product(rows, bucket_w) + bucket_b
    bias = relative_bias(bucket_table(buckets), relative)
    mixed, logsum = attend(
        query.reshape(head_shape),
        keys.reshape(head_shape),
        values.reshape(head_shape),
        bias,
        allowed,
    )
    mixed = mixed.reshape(rows.shape)
    sum_first = rows + product(mixed, self_o) + self_ob
    first = layer_norm(sum_first, gain_a, shift_a)
    first_low = first.astype(jnp.bfloat16)
    probe = (product(first_low, cross_q) + cross_qb).astype(jnp.bfloat16)
    index = product(enc_rows, cross_k).astype(jnp.bfloat16)
    content = (product(enc_rows, cross_v) + cross_vb).astype(jnp.bfloat16)
    joined, cross_logsum = attend(
        probe.reshape(head_shape),
        index.reshape(source_shape),
        content.reshape(source_shape),
        0.0,
        True,
    )
    joined = joined.reshape(rows.shape)
    sum_second = first + product(joined, cross_o) + cross_ob
    second = layer_norm(sum_second, gain_b, shift_b)
    second_low = second.astype(jnp.bfloat16)
    before = product(second_low, ffn_in) + ffn_inb
    activity = jax.nn.gelu(before, approximate=False).astype(jnp.bfloat16)
    sum_third = second + product(activity, ffn_out) + ffn_outb
    third = layer_norm(sum_third, gain_c, shift_c)
    kept = (
        rows,
        enc_rows,
        query,
        keys,
        values,
        relative,
        logsum,
        mixed,
        sum_first,
        first_low,
        probe,
        index,
        content,
        cross_logsum,
        joined,
        sum_second,
        second_low,
        before,
        activity,
        sum_third,
    )
    return (third, kept)


def backward(whole, kept, cotangent, buckets, lengths):
    (
        self_q,
        self_qb,
        self_k,
        self_v,
        self_vb,
        self_o,
        self_ob,
        bucket_w,
        bucket_b,
        cross_q,
        cross_qb,
        cross_k,
        cross_v,
        cross_vb,
        cross_o,
        cross_ob,
        ffn_in,
        ffn_inb,
        ffn_out,
        ffn_outb,
        gain_a,
        shift_a,
        gain_b,
        shift_b,
        gain_c,
        shift_c,
    ) = whole
    (
        rows,
        enc_rows,
        query,
        keys,
        values,
        relative,
        logsum,
        mixed,
        sum_first,
        first_low,
        probe,
        index,
        content,
        cross_logsum,
        joined,
        sum_second,
        second_low,
        before,
        activity,
        sum_third,
    ) = kept
    count, streams, target, width = cotangent.shape
    source = enc_rows.shape[0] // count
    head_shape = (count, streams * target, width // HEAD_DIM, HEAD_DIM)
    source_shape = (count, source, width // HEAD_DIM, HEAD_DIM)
    allowed = visible(target)
    grad_third = (
        cotangent.reshape(rows.shape).astype(jnp.float32) * valid_rows(lengths, target)[:, None]
    )
    grad_sum_third, grad_gain_c, grad_shift_c = norm_back(sum_third, gain_c, shift_c, grad_third)
    branch_three = grad_sum_third.astype(jnp.bfloat16)
    grad_ffn_out = product_left(activity, branch_three)
    grad_ffn_outb = column_sum(branch_three)
    share_three = (
        lax.psum_scatter(grad_ffn_out, ("dp", "fsdp"), scatter_dimension=0, tiled=True),
        lax.psum_scatter(grad_ffn_outb, ("dp", "fsdp"), scatter_dimension=0, tiled=True),
        lax.psum_scatter(grad_gain_c, ("dp", "fsdp"), scatter_dimension=0, tiled=True),
        lax.psum_scatter(grad_shift_c, ("dp", "fsdp"), scatter_dimension=0, tiled=True),
    )
    unused, gelu_pull = jax.vjp(partial(jax.nn.gelu, approximate=False), before)
    grad_before = gelu_pull(product_right(branch_three, ffn_out))[0].astype(jnp.bfloat16)
    grad_ffn_in = product_left(second_low, grad_before)
    grad_ffn_inb = column_sum(grad_before)
    grad_second = grad_sum_third + product_right(grad_before, ffn_in)
    grad_sum_second, grad_gain_b, grad_shift_b = norm_back(sum_second, gain_b, shift_b, grad_second)
    share_two = (
        lax.psum_scatter(grad_ffn_in, ("dp", "fsdp"), scatter_dimension=0, tiled=True),
        lax.psum_scatter(grad_ffn_inb, ("dp", "fsdp"), scatter_dimension=0, tiled=True),
        lax.psum_scatter(grad_gain_b, ("dp", "fsdp"), scatter_dimension=0, tiled=True),
        lax.psum_scatter(grad_shift_b, ("dp", "fsdp"), scatter_dimension=0, tiled=True),
    )
    branch_two = grad_sum_second.astype(jnp.bfloat16)
    grad_cross_o = product_left(joined, branch_two)
    grad_cross_ob = column_sum(branch_two)
    grad_joined = product_right(branch_two, cross_o).astype(jnp.bfloat16)
    unused, grad_probe, grad_index, grad_content = attend_back(
        probe.reshape(head_shape),
        index.reshape(source_shape),
        content.reshape(source_shape),
        0.0,
        True,
        cross_logsum,
        grad_joined.reshape(head_shape),
    )
    grad_probe = grad_probe.reshape(rows.shape)
    grad_index = grad_index.reshape(enc_rows.shape)
    grad_content = grad_content.reshape(enc_rows.shape)
    grad_cross_q = product_left(first_low, grad_probe)
    grad_cross_qb = column_sum(grad_probe)
    grad_cross_k = product_left(enc_rows, grad_index)
    grad_cross_v = product_left(enc_rows, grad_content)
    grad_cross_vb = column_sum(grad_content)
    share_cross = (
        lax.psum_scatter(grad_cross_q, ("dp", "fsdp"), scatter_dimension=0, tiled=True),
        lax.psum_scatter(grad_cross_qb, ("dp", "fsdp"), scatter_dimension=0, tiled=True),
        lax.psum_scatter(grad_cross_k, ("dp", "fsdp"), scatter_dimension=0, tiled=True),
        lax.psum_scatter(grad_cross_v, ("dp", "fsdp"), scatter_dimension=0, tiled=True),
        lax.psum_scatter(grad_cross_vb, ("dp", "fsdp"), scatter_dimension=0, tiled=True),
        lax.psum_scatter(grad_cross_o, ("dp", "fsdp"), scatter_dimension=0, tiled=True),
        lax.psum_scatter(grad_cross_ob, ("dp", "fsdp"), scatter_dimension=0, tiled=True),
    )
    grad_encoded = product_right(grad_index, cross_k) + product_right(grad_content, cross_v)
    grad_first = grad_sum_second + product_right(grad_probe, cross_q)
    grad_sum_first, grad_gain_a, grad_shift_a = norm_back(sum_first, gain_a, shift_a, grad_first)
    branch_one = grad_sum_first.astype(jnp.bfloat16)
    grad_self_o = product_left(mixed, branch_one)
    grad_self_ob = column_sum(branch_one)
    grad_mixed = product_right(branch_one, self_o).astype(jnp.bfloat16)
    onehot = bucket_table(buckets)
    bias = relative_bias(onehot, relative)
    grad_scores, grad_query, grad_keys, grad_values = attend_back(
        query.reshape(head_shape),
        keys.reshape(head_shape),
        values.reshape(head_shape),
        bias,
        allowed,
        logsum,
        grad_mixed.reshape(head_shape),
    )
    grad_relative = jnp.einsum(
        "nqbk,nhqk->nqhb", onehot, grad_scores.astype(jnp.float32), precision=lax.Precision.HIGHEST
    )
    grad_relative = grad_relative.reshape(rows.shape[0], -1).astype(jnp.bfloat16)
    grad_query = grad_query.reshape(rows.shape)
    grad_keys = grad_keys.reshape(rows.shape)
    grad_values = grad_values.reshape(rows.shape)
    grad_self_q = product_left(rows, grad_query)
    grad_self_qb = column_sum(grad_query)
    grad_self_k = product_left(rows, grad_keys)
    grad_self_v = product_left(rows, grad_values)
    grad_self_vb = column_sum(grad_values)
    grad_bucket_w = product_left(rows, grad_relative)
    grad_bucket_b = column_sum(grad_relative)
    grad_tokens = (
        grad_sum_first
        + product_right(grad_query, self_q)
        + product_right(grad_keys, self_k)
        + product_right(grad_values, self_v)
        + product_right(grad_relative, bucket_w)
    )
    share_one = (
        lax.psum_scatter(grad_self_q, ("dp", "fsdp"), scatter_dimension=0, tiled=True),
        lax.psum_scatter(grad_self_qb, ("dp", "fsdp"), scatter_dimension=0, tiled=True),
        lax.psum_scatter(grad_self_k, ("dp", "fsdp"), scatter_dimension=0, tiled=True),
        lax.psum_scatter(grad_self_v, ("dp", "fsdp"), scatter_dimension=0, tiled=True),
        lax.psum_scatter(grad_self_vb, ("dp", "fsdp"), scatter_dimension=0, tiled=True),
        lax.psum_scatter(grad_self_o, ("dp", "fsdp"), scatter_dimension=0, tiled=True),
        lax.psum_scatter(grad_self_ob, ("dp", "fsdp"), scatter_dimension=0, tiled=True),
        lax.psum_scatter(grad_bucket_w, ("dp", "fsdp"), scatter_dimension=0, tiled=True),
        lax.psum_scatter(grad_bucket_b, ("dp", "fsdp"), scatter_dimension=0, tiled=True),
        lax.psum_scatter(grad_gain_a, ("dp", "fsdp"), scatter_dimension=0, tiled=True),
        lax.psum_scatter(grad_shift_a, ("dp", "fsdp"), scatter_dimension=0, tiled=True),
    )
    shares = (
        share_one[0],
        share_one[1],
        share_one[2],
        share_one[3],
        share_one[4],
        share_one[5],
        share_one[6],
        share_one[7],
        share_one[8],
        share_cross[0],
        share_cross[1],
        share_cross[2],
        share_cross[3],
        share_cross[4],
        share_cross[5],
        share_cross[6],
        share_two[0],
        share_two[1],
        share_three[0],
        share_three[1],
        share_one[9],
        share_one[10],
        share_two[2],
        share_two[3],
        share_three[2],
        share_three[3],
    )
    return (
        shares,
        grad_tokens.reshape(cotangent.shape),
        grad_encoded.reshape(count, source, width),
    )


def per_device(
    tokens,
    encoded,
    cotangent,
    buckets,
    lengths,
    self_q,
    self_qb,
    self_k,
    self_v,
    self_vb,
    self_o,
    self_ob,
    bucket_w,
    bucket_b,
    cross_q,
    cross_qb,
    cross_k,
    cross_v,
    cross_vb,
    cross_o,
    cross_ob,
    ffn_in,
    ffn_inb,
    ffn_out,
    ffn_outb,
    gain_a,
    shift_a,
    gain_b,
    shift_b,
    gain_c,
    shift_c,
):
    whole = (
        lax.all_gather(self_q, ("dp", "fsdp"), axis=0, tiled=True),
        lax.all_gather(self_qb, ("dp", "fsdp"), axis=0, tiled=True),
        lax.all_gather(self_k, ("dp", "fsdp"), axis=0, tiled=True),
        lax.all_gather(self_v, ("dp", "fsdp"), axis=0, tiled=True),
        lax.all_gather(self_vb, ("dp", "fsdp"), axis=0, tiled=True),
        lax.all_gather(self_o, ("dp", "fsdp"), axis=0, tiled=True),
        lax.all_gather(self_ob, ("dp", "fsdp"), axis=0, tiled=True),
        lax.all_gather(bucket_w, ("dp", "fsdp"), axis=0, tiled=True),
        lax.all_gather(bucket_b, ("dp", "fsdp"), axis=0, tiled=True),
        lax.all_gather(cross_q, ("dp", "fsdp"), axis=0, tiled=True),
        lax.all_gather(cross_qb, ("dp", "fsdp"), axis=0, tiled=True),
        lax.all_gather(cross_k, ("dp", "fsdp"), axis=0, tiled=True),
        lax.all_gather(cross_v, ("dp", "fsdp"), axis=0, tiled=True),
        lax.all_gather(cross_vb, ("dp", "fsdp"), axis=0, tiled=True),
        lax.all_gather(cross_o, ("dp", "fsdp"), axis=0, tiled=True),
        lax.all_gather(cross_ob, ("dp", "fsdp"), axis=0, tiled=True),
        lax.all_gather(ffn_in, ("dp", "fsdp"), axis=0, tiled=True),
        lax.all_gather(ffn_inb, ("dp", "fsdp"), axis=0, tiled=True),
        lax.all_gather(ffn_out, ("dp", "fsdp"), axis=0, tiled=True),
        lax.all_gather(ffn_outb, ("dp", "fsdp"), axis=0, tiled=True),
        lax.all_gather(gain_a, ("dp", "fsdp"), axis=0, tiled=True),
        lax.all_gather(shift_a, ("dp", "fsdp"), axis=0, tiled=True),
        lax.all_gather(gain_b, ("dp", "fsdp"), axis=0, tiled=True),
        lax.all_gather(shift_b, ("dp", "fsdp"), axis=0, tiled=True),
        lax.all_gather(gain_c, ("dp", "fsdp"), axis=0, tiled=True),
        lax.all_gather(shift_c, ("dp", "fsdp"), axis=0, tiled=True),
    )
    third, kept = forward(whole, tokens, encoded, buckets)
    outputs = (
        (third * valid_rows(lengths, tokens.shape[2])[:, None])
        .reshape(tokens.shape)
        .astype(jnp.bfloat16)
    )
    shares, grad_tokens, grad_encoded = backward(whole, kept, cotangent, buckets, lengths)
    return (
        outputs,
        grad_tokens,
        grad_encoded,
        shares[0],
        shares[1],
        shares[2],
        shares[3],
        shares[4],
        shares[5],
        shares[6],
        shares[7],
        shares[8],
        shares[9],
        shares[10],
        shares[11],
        shares[12],
        shares[13],
        shares[14],
        shares[15],
        shares[16],
        shares[17],
        shares[18],
        shares[19],
        shares[20],
        shares[21],
        shares[22],
        shares[23],
        shares[24],
        shares[25],
    )


def solution(mesh):
    placed = (
        P(("dp", "fsdp"), None, None, None),
        P(("dp", "fsdp"), None, None),
        P(("dp", "fsdp"), None, None, None),
        P(("dp", "fsdp"), None, None, None),
        P(("dp", "fsdp")),
        P(("dp", "fsdp"), None),
        P(("dp", "fsdp")),
        P(("dp", "fsdp"), None),
        P(("dp", "fsdp"), None),
        P(("dp", "fsdp")),
        P(("dp", "fsdp"), None),
        P(("dp", "fsdp")),
        P(("dp", "fsdp"), None),
        P(("dp", "fsdp")),
        P(("dp", "fsdp"), None),
        P(("dp", "fsdp")),
        P(("dp", "fsdp"), None),
        P(("dp", "fsdp"), None),
        P(("dp", "fsdp")),
        P(("dp", "fsdp"), None),
        P(("dp", "fsdp")),
        P(("dp", "fsdp"), None),
        P(("dp", "fsdp")),
        P(("dp", "fsdp"), None),
        P(("dp", "fsdp")),
        P(("dp", "fsdp")),
        P(("dp", "fsdp")),
        P(("dp", "fsdp")),
        P(("dp", "fsdp")),
        P(("dp", "fsdp")),
        P(("dp", "fsdp")),
    )
    return jax.shard_map(
        per_device,
        mesh=mesh,
        in_specs=placed,
        out_specs=(
            P(("dp", "fsdp"), None, None, None),
            P(("dp", "fsdp"), None, None, None),
            P(("dp", "fsdp"), None, None),
            P(("dp", "fsdp"), None),
            P(("dp", "fsdp")),
            P(("dp", "fsdp"), None),
            P(("dp", "fsdp"), None),
            P(("dp", "fsdp")),
            P(("dp", "fsdp"), None),
            P(("dp", "fsdp")),
            P(("dp", "fsdp"), None),
            P(("dp", "fsdp")),
            P(("dp", "fsdp"), None),
            P(("dp", "fsdp")),
            P(("dp", "fsdp"), None),
            P(("dp", "fsdp"), None),
            P(("dp", "fsdp")),
            P(("dp", "fsdp"), None),
            P(("dp", "fsdp")),
            P(("dp", "fsdp"), None),
            P(("dp", "fsdp")),
            P(("dp", "fsdp"), None),
            P(("dp", "fsdp")),
            P(("dp", "fsdp")),
            P(("dp", "fsdp")),
            P(("dp", "fsdp")),
            P(("dp", "fsdp")),
            P(("dp", "fsdp")),
            P(("dp", "fsdp")),
        ),
        check_vma=False,
    )
```

profile of v0, /device:TPU:0, one launch (start us, length us, event | category | flops | bytes accessed | tf_op | source)
XLA Modules:
  0.0 2908.8 jit_solution(17157720682645126500)
XLA Ops:
  26.5 42.5 %all-reduce.30 = (bf16[1024]{0:T(1024)(128)(2,1)S(1)}, bf16[1024]{0:T(1024)(128)(2,1)S(1)}, bf16[1024]{0:T(1024)(128)(2,1)S(1)}, bf16[512]{0:T(512)(128)(2,1)S(1...) all-reduce(bf16[1024]{0:T(1024)(128)(2,1)S(1)} %dynamic-update-slic, ...), channel_id=1, replica_groups=mesh['dp'=16,'fsdp'=2] {'dp','fsdp'}, use_global_device_ids=true, to_apply=%add.6 | all-reduce | flops 13824 | bytes 55296
  69.0 65.8 %all-gather = bf16[32,1,128]{2,1,0:T(2,128)(2,1)S(1)} all-gather(bf16[1,1,128]{2,1,0:T(2,128)(2,1)} %bitcast.264), channel_id=1, replica_groups=mesh['dp'=16,'fsdp'=2] {'dp','fsdp'}, dimensions={0}, use_global_device_ids=true | all-gather | bytes 8448 | tf_op jit(solution)/shard_map/all_gather | solution.py:455
  142.9 4.7 fusion.1
  147.6 5.3 copy.116
  152.8 2.9 add_convert_fusion.1
  157.1 27.3 all-gather.13.cloned.1.call-done
  186.9 55.7 %all-gather.15.cloned.1.call-done = bf16[1024,1024]{1,0:T(8,128)(2,1)} async-done(((bf16[32,1024]{1,0:T(8,128)(2,1)}), bf16[1024,1024]{1,0:T(8,128)(2,1)}) %all-gather.15.cloned.1.call-update) | async-done | bytes 2097168 | tf_op jit(solution)/shard_map/all_gather | solution.py:438
  245.1 55.7 %all-gather.17.cloned.1.call-done = bf16[1024,1024]{1,0:T(8,128)(2,1)} async-done(((bf16[32,1024]{1,0:T(8,128)(2,1)}), bf16[1024,1024]{1,0:T(8,128)(2,1)}) %all-gather.17.cloned.1.call-update) | async-done | bytes 2097168 | tf_op jit(solution)/shard_map/all_gather | solution.py:440
  300.8 3.1 convolution_convert_fusion.7
  305.2 3.4 fusion.55
  311.3 47.7 %all-gather.21.cloned.1.call-done = bf16[1024,1024]{1,0:T(8,128)(2,1)} async-done(((bf16[32,1024]{1,0:T(8,128)(2,1)}), bf16[1024,1024]{1,0:T(8,128)(2,1)}) %all-gather.21.cloned.1.call-update) | async-done | bytes 2097168 | tf_op jit(solution)/shard_map/all_gather | solution.py:443
  359.0 2.4 fusion.56
  361.7 55.7 %all-gather.25.cloned.1.call-done = bf16[1024,1024]{1,0:T(8,128)(2,1)} async-done(((bf16[32,1024]{1,0:T(8,128)(2,1)}), bf16[1024,1024]{1,0:T(8,128)(2,1)}) %all-gather.25.cloned.1.call-update) | async-done | bytes 2097168 | tf_op jit(solution)/shard_map/all_gather | solution.py:447
  417.4 3.1 fusion.23
  422.6 53.2 %all-gather.27.cloned.1.call-done = bf16[1024,1024]{1,0:T(8,128)(2,1)} async-done(((bf16[32,1024]{1,0:T(8,128)(2,1)}), bf16[1024,1024]{1,0:T(8,128)(2,1)}) %all-gather.27.cloned.1.call-update) | async-done | bytes 2097168 | tf_op jit(solution)/shard_map/all_gather | solution.py:449
  475.7 3.8 convolution_convert_fusion.1
  481.8 2.8 multiply_reduce_fusion.1
  487.8 2.7 convolution_convert_fusion.2
  490.5 43.6 %all-gather.29.cloned.1.call-done = bf16[1024,1024]{1,0:T(8,128)(2,1)} async-done(((bf16[32,1024]{1,0:T(8,128)(2,1)}), bf16[1024,1024]{1,0:T(8,128)(2,1)}) %all-gather.29.cloned.1.call-update) | async-done | bytes 2097168 | tf_op jit(solution)/shard_map/all_gather | solution.py:452
  534.1 2.6 fusion.57
  538.0 75.1 %all-gather.31.cloned.1.call-done = bf16[1024,4096]{1,0:T(8,128)(2,1)} async-done(((bf16[32,4096]{1,0:T(8,128)(2,1)}), bf16[1024,4096]{1,0:T(8,128)(2,1)}) %all-gather.31.cloned.1.call-update) | async-done | bytes 8388624 | tf_op jit(solution)/shard_map/all_gather | solution.py:454
  613.1 16.3 multiply_convert_fusion.1
  629.4 62.7 %all-gather.33.cloned.1.call-done = bf16[4096,1024]{1,0:T(8,128)(2,1)} async-done(((bf16[128,1024]{1,0:T(8,128)(2,1)}), bf16[4096,1024]{1,0:T(8,128)(2,1)}) %all-gather.33.cloned.1.call-update) | async-done | bytes 8388624 | tf_op jit(solution)/shard_map/all_gather | solution.py:456
  692.1 6.7 fusion.58
  702.4 12.1 convert_reduce_fusion
  715.8 6.7 multiply_reduce_fusion.4
  729.2 6.9 multiply_reduce_fusion
  750.4 3.7 fusion.6
  759.5 4.6 copy.126
  764.0 6.3 convert_reduce_fusion.1
  770.4 2.5 convert_reduce_fusion.2
  780.0 2.9 copy.144
  783.1 3.7 convolution_bitcast_fusion.4
  786.8 5.6 copy.138
  792.5 2.5 fusion.25
  795.8 2.7 convolution_bitcast_fusion.3
  798.5 5.4 copy.140
  804.0 3.7 convolution_bitcast_fusion.2
  807.7 5.3 copy.142
  814.0 2.6 fusion.60
  817.7 2.9 fusion.48
  820.8 3.0 multiply_convert_fusion.2
  824.8 3.2 convolution_bitcast_fusion.1
  828.0 5.4 copy.146
  834.6 3.2 convolution_bitcast_fusion
  837.8 5.4 copy.148
  844.4 2.7 fusion.61
  848.3 9.8 fusion.45
  859.7 9.2 fusion.62
  870.2 2.5 convolution_add_fusion.4
  872.7 2.5 convolution_add_fusion.3
  879.4 2.7 add_bitcast_fusion
  882.1 26.7 all-reduce.33.cloned.1.call-done
  927.6 124.0 %reduce-scatter.40.cloned.1.call-done = f32[32,512]{1,0:T(8,128)} async-done(((f32[1024,512]{1,0:T(8,128)}), f32[32,512]{1,0:T(8,128)}) %reduce-scatter.40.cloned.1.call-update) | async-done | bytes 65552
  1051.6 140.6 %reduce-scatter.34.cloned.1.call-done = f32[32,1024]{1,0:T(8,128)} async-done(((f32[1024,1024]{1,0:T(8,128)}), f32[32,1024]{1,0:T(8,128)}) %reduce-scatter.34.cloned.1.call-update) | async-done | bytes 131088
  1192.2 141.3 %reduce-scatter.36.cloned.1.call-done = f32[32,1024]{1,0:T(8,128)} async-done(((f32[1024,1024]{1,0:T(8,128)}), f32[32,1024]{1,0:T(8,128)}) %reduce-scatter.36.cloned.1.call-update) | async-done | bytes 131088
  1333.5 141.6 %reduce-scatter.38.cloned.1.call-done = f32[32,1024]{1,0:T(8,128)} async-done(((f32[1024,1024]{1,0:T(8,128)}), f32[32,1024]{1,0:T(8,128)}) %reduce-scatter.38.cloned.1.call-update) | async-done | bytes 131088
  1475.1 141.5 %reduce-scatter.24.cloned.1.call-done = f32[32,1024]{1,0:T(8,128)} async-done(((f32[1024,1024]{1,0:T(8,128)}), f32[32,1024]{1,0:T(8,128)}) %reduce-scatter.24.cloned.1.call-update) | async-done | bytes 131088 | tf_op jit(solution)/shard_map/reduce_scatter | solution.py:362
  1616.6 141.8 %reduce-scatter.26.cloned.1.call-done = f32[32,1024]{1,0:T(8,128)} async-done(((f32[1024,1024]{1,0:T(8,128)}), f32[32,1024]{1,0:T(8,128)}) %reduce-scatter.26.cloned.1.call-update) | async-done | bytes 131088 | tf_op jit(solution)/shard_map/reduce_scatter | solution.py:309
  1758.4 141.3 %reduce-scatter.42.cloned.1.call-done = f32[32,1024]{1,0:T(8,128)} async-done(((f32[1024,1024]{1,0:T(8,128)}), f32[32,1024]{1,0:T(8,128)}) %reduce-scatter.42.cloned.1.call-update) | async-done | bytes 131088
  1899.7 142.1 %reduce-scatter.44.cloned.1.call-done = f32[32,1024]{1,0:T(8,128)} async-done(((f32[1024,1024]{1,0:T(8,128)}), f32[32,1024]{1,0:T(8,128)}) %reduce-scatter.44.cloned.1.call-update) | async-done | bytes 131088
  2041.7 141.4 %reduce-scatter.28.cloned.1.call-done = f32[32,1024]{1,0:T(8,128)} async-done(((f32[1024,1024]{1,0:T(8,128)}), f32[32,1024]{1,0:T(8,128)}) %reduce-scatter.28.cloned.1.call-update) | async-done | bytes 131088 | tf_op jit(solution)/shard_map/reduce_scatter | solution.py:314
  2183.2 357.1 %reduce-scatter.30.cloned.1.call-done = f32[32,4096]{1,0:T(8,128)} async-done(((f32[1024,4096]{1,0:T(8,128)}), f32[32,4096]{1,0:T(8,128)}) %reduce-scatter.30.cloned.1.call-update) | async-done | bytes 524304 | tf_op jit(solution)/shard_map/reduce_scatter | solution.py:282
  2540.2 361.7 %reduce-scatter.32.cloned.1.call-done = f32[128,1024]{1,0:T(8,128)} async-done(((f32[4096,1024]{1,0:T(8,128)}), f32[128,1024]{1,0:T(8,128)}) %reduce-scatter.32.cloned.1.call-update) | async-done | bytes 524304 | tf_op jit(solution)/shard_map/reduce_scatter | solution.py:270
  (277 shorter events, 117.4 us)
Async XLA Ops:
  7.2 145.6 %copy-start = (bf16[1,512,1024]{2,1,0:T(8,128)(2,1)S(1)}, bf16[1,512,1024]{2,1,0:T(8,128)(2,1)}, u32[]{:S(2)}) copy-start(bf16[1,512,1024]{2,1,0:T(8,128)(2,1)} %param.32) | copy-start | bytes 3145732
  7.2 135.6 %copy-start.47 = (s32[1,2,128,256]{3,2,1,0:T(8,128)S(1)}, s32[1,2,128,256]{3,2,1,0:T(8,128)}, u32[]{:S(2)}) copy-start(s32[1,2,128,256]{3,2,1,0:T(8,128)} %param.34) | copy-start | bytes 786436
  7.2 130.5 %all-gather.19.cloned.1.call-start = ((), (), s32[]{:S(2)}) async-start(), calls=%async_computation.14 | async-start | bytes 1081344 | tf_op jit(solution)/shard_map/all_gather | solution.py:445
  8.0 144.9 %all-gather.23.cloned.1.call-start = ((), (), s32[]{:S(2)}) async-start(), calls=%async_computation.16 | async-start | bytes 2162688 | tf_op jit(solution)/shard_map/all_gather | solution.py:450
  8.7 175.7 %all-gather.13.cloned.1.call-start = ((), (), s32[]{:S(2)}) async-start(), calls=%async_computation.11 | async-start | bytes 2162688 | tf_op jit(solution)/shard_map/all_gather | solution.py:441
  9.4 233.2 %all-gather.15.cloned.1.call-start = ((), (), s32[]{:S(2)}) async-start(), calls=%async_computation.12 | async-start | bytes 2162688 | tf_op jit(solution)/shard_map/all_gather | solution.py:438
  10.0 290.8 %all-gather.17.cloned.1.call-start = ((), (), s32[]{:S(2)}) async-start(), calls=%async_computation.13 | async-start | bytes 2162688 | tf_op jit(solution)/shard_map/all_gather | solution.py:440
  10.6 348.4 %all-gather.21.cloned.1.call-start = ((), (), s32[]{:S(2)}) async-start(), calls=%async_computation.15 | async-start | bytes 2162688 | tf_op jit(solution)/shard_map/all_gather | solution.py:443
  11.2 406.2 %all-gather.25.cloned.1.call-start = ((), (), s32[]{:S(2)}) async-start(), calls=%async_computation.17 | async-start | bytes 2162688 | tf_op jit(solution)/shard_map/all_gather | solution.py:447
  11.9 463.8 %all-gather.27.cloned.1.call-start = ((), (), s32[]{:S(2)}) async-start(), calls=%async_computation.18 | async-start | bytes 2162688 | tf_op jit(solution)/shard_map/all_gather | solution.py:449
  12.7 521.4 %all-gather.29.cloned.1.call-start = ((), (), s32[]{:S(2)}) async-start(), calls=%async_computation.19 | async-start | bytes 2162688 | tf_op jit(solution)/shard_map/all_gather | solution.py:452
  13.4 599.7 %all-gather.31.cloned.1.call-start = ((), (), s32[]{:S(2)}) async-start(), calls=%async_computation.20 | async-start | bytes 8650752 | tf_op jit(solution)/shard_map/all_gather | solution.py:454
  14.0 678.1 %all-gather.33.cloned.1.call-start = ((), (), s32[]{:S(2)}) async-start(), calls=%async_computation.21 | async-start | bytes 8650752 | tf_op jit(solution)/shard_map/all_gather | solution.py:456
  14.7 894.0 %all-reduce.33.cloned.1.call-start = ((), (), s32[]{:S(2)}) async-start(), calls=%async_computation.33 | async-start | bytes 143360
  152.8 31.5 %copy-start.6 = (bf16[1,2,128,1024]{3,2,1,0:T(8,128)(2,1)S(1)}, bf16[1,2,128,1024]{3,2,1,0:T(8,128)(2,1)}, u32[]{:S(2)}) copy-start(bf16[1,2,128,1024]{3,2,1,0:T(8,128)(2,1)} %param.31) | copy-start | bytes 1572868
  186.9 122.3 %copy-start.21 = (bf16[256,1024]{0,1:T(8,128)(2,1)}, bf16[256,1024]{0,1:T(8,128)(2,1)S(1)}, u32[]{:S(2)}) copy-start(bf16[256,1024]{0,1:T(8,128)(2,1)S(1)} %copy.111) | copy-start | bytes 1572868
  245.1 63.4 %copy-start.24 = (bf16[256,1024]{0,1:T(8,128)(2,1)}, bf16[256,1024]{0,1:T(8,128)(2,1)S(1)}, u32[]{:S(2)}) copy-start(bf16[256,1024]{0,1:T(8,128)(2,1)S(1)} %copy.112) | copy-start | bytes 1572868
  305.1 3.4 copy-start.25
  308.5 2.0 copy-start.2
  484.6 3.2 copy-start.1
  484.6 3.2 copy-start.12
  692.1 7.0 copy-start.23
  698.9 3.5 copy-start.50
  702.4 12.1 copy-start.35
  702.4 13.5 copy-start.8
  714.5 1.3 copy-start.42
  722.6 3.0 copy-start.40
  729.2 6.9 slice-start
  729.2 6.9 slice-start.1
  736.1 2.4 copy-start.13
  738.5 5.3 copy-start.4
  738.5 2.0 copy-start.15
  738.5 3.6 copy-start.41
  739.9 4.3 copy-start.28
  742.1 4.7 copy-start.32
  750.4 3.7 copy-start.3
  750.4 3.9 copy-start.22
  755.8 2.3 copy-start.26
  756.8 1.3 copy-start.5
  764.0 6.4 copy-start.34
  778.2 273.4 %reduce-scatter.40.cloned.1.call-start = ((), (), s32[]{:S(2)}) async-start(), calls=%async_computation.30 | async-start | bytes 2162688
  783.0 409.2 %reduce-scatter.34.cloned.1.call-start = ((), (), s32[]{:S(2)}) async-start(), calls=%async_computation.27 | async-start | bytes 4325376
  792.4 541.1 %reduce-scatter.36.cloned.1.call-start = ((), (), s32[]{:S(2)}) async-start(), calls=%async_computation.28 | async-start | bytes 4325376
  803.9 671.2 %reduce-scatter.38.cloned.1.call-start = ((), (), s32[]{:S(2)}) async-start(), calls=%async_computation.29 | async-start | bytes 4325376
  813.0 803.6 %reduce-scatter.24.cloned.1.call-start = ((), (), s32[]{:S(2)}) async-start(), calls=%async_computation.22 | async-start | bytes 4325376 | tf_op jit(solution)/shard_map/reduce_scatter | solution.py:362
  816.7 4.0 copy-start.27
  816.7 941.7 %reduce-scatter.26.cloned.1.call-start = ((), (), s32[]{:S(2)}) async-start(), calls=%async_computation.23 | async-start | bytes 4325376 | tf_op jit(solution)/shard_map/reduce_scatter | solution.py:309
  820.7 1079.0 %reduce-scatter.42.cloned.1.call-start = ((), (), s32[]{:S(2)}) async-start(), calls=%async_computation.31 | async-start | bytes 4325376
  833.4 1.2 copy-start.45
  833.4 1208.4 %reduce-scatter.44.cloned.1.call-start = ((), (), s32[]{:S(2)}) async-start(), calls=%async_computation.32 | async-start | bytes 4325376
  843.2 1340.0 %reduce-scatter.28.cloned.1.call-start = ((), (), s32[]{:S(2)}) async-start(), calls=%async_computation.24 | async-start | bytes 4325376 | tf_op jit(solution)/shard_map/reduce_scatter | solution.py:314
  847.0 1.2 copy-start.9
  847.1 1693.1 %reduce-scatter.30.cloned.1.call-start = ((), (), s32[]{:S(2)}) async-start(), calls=%async_computation.25 | async-start | bytes 17301504 | tf_op jit(solution)/shard_map/reduce_scatter | solution.py:282
  858.1 1.6 copy-start.31
  858.1 2043.7 %reduce-scatter.32.cloned.1.call-start = ((), (), s32[]{:S(2)}) async-start(), calls=%async_computation.26 | async-start | bytes 17301504 | tf_op jit(solution)/shard_map/reduce_scatter | solution.py:270
  868.9 1.4 copy-start.17
  868.9 3.8 copy-start.19
  870.2 5.0 copy-start.16
  870.2 5.0 copy-start.33
  872.7 3.3 copy-start.30
  875.2 2.3 copy-start.44
  875.2 2.3 copy-start.49
  877.5 1.3 copy-start.46
  877.5 1.9 copy-start.48
  (12 other events, 11.9 us)
Sparse Core Ops, SparseCore 0:
  10.9 56.5 all-gather.18
  70.5 55.4 all-gather.22
  129.0 55.3 all-gather.12
  187.2 55.3 all-gather.14
  245.4 55.3 all-gather.16
  303.6 55.3 all-gather.20
  362.0 55.3 all-gather.24
  420.4 55.3 all-gather.26
  478.7 55.3 all-gather.28
  536.9 76.1 all-gather.30
  616.1 75.9 all-gather.32
  778.3 130.3 all-reduce.32
  911.6 140.0 reduce-scatter.39
  1054.4 137.7 reduce-scatter.33
  1195.0 138.4 reduce-scatter.35
  1336.3 138.7 reduce-scatter.37
  1477.9 138.6 reduce-scatter.23
  1619.4 138.9 reduce-scatter.25
  1761.3 138.2 reduce-scatter.41
  1902.5 139.2 reduce-scatter.43
  2044.7 138.4 reduce-scatter.27
  2186.1 354.0 reduce-scatter.29
  2543.2 358.6 reduce-scatter.31
where the time goes:
time: 2920 us; the launch traced here: 2910 us
  waiting for transfers between devices  2480 us (85%)
  matrix products  172 us (6%)
  local copies, waits for them, and re-layouts  113 us (4%)
  blocking collectives  108 us (4%)
    unnamed x30, waiting for transfers between devices  865 us
    reduce_scatter x1, waiting for transfers between devices, backward(): lax.psum_scatter(grad_ffn_out, ('dp', 'fsdp'), scatter_dimension=0, tiled...  362 us
    reduce_scatter x1, waiting for transfers between devices, backward(): lax.psum_scatter(grad_ffn_in, ('dp', 'fsdp'), scatter_dimension=0, tiled=...  357 us
    reduce_scatter x1, waiting for transfers between devices, backward(): lax.psum_scatter(grad_cross_q, ('dp', 'fsdp'), scatter_dimension=0, tiled...  142 us
    reduce_scatter x1, waiting for transfers between devices, backward(): lax.psum_scatter(grad_self_o, ('dp', 'fsdp'), scatter_dimension=0, tiled=...  141 us
    reduce_scatter x1, waiting for transfers between devices, backward(): lax.psum_scatter(grad_cross_o, ('dp', 'fsdp'), scatter_dimension=0, tiled...  141 us
    unnamed x155, local copies, waits for them, and re-layouts  82.8 us
    all_gather x1, waiting for transfers between devices, per_device(): lax.all_gather(ffn_in, ('dp', 'fsdp'), axis=0, tiled=True)  75.1 us
  transfers between devices with their start and end apart: 23, of which 21 were waited for; matrix products, arithmetic and copies ran while one was open for 7% of the time, Pallas kernels for 0%

commit v1 on v0

v1 whole, which is shorter than its diff:
```python
from functools import partial

import jax
import jax.numpy as jnp
from jax import lax
from jax.experimental import pallas as pl
from jax.experimental.pallas import tpu as pltpu
from jax.sharding import PartitionSpec as P

HEAD_DIM = 64
BUCKETS = 32
CORES = 2
ROWS = 32
WIDE = 1024
AHEAD = 3
LINES = 64
LAG = 2
AXES = ("dp", "fsdp")
(
    SELF_Q, SELF_K, SELF_V, BUCKET_W, SELF_O, CROSS_K,
    CROSS_V, CROSS_Q, CROSS_O, FFN_IN, FFN_OUT,
) = MATRICES = tuple(range(11))
(
    SELF_QB, SELF_VB, SELF_OB, CROSS_QB, CROSS_VB, CROSS_OB,
    FFN_OUTB, GAIN_A, SHIFT_A, GAIN_B, SHIFT_B, GAIN_C,
    SHIFT_C, BUCKET_B, FFN_INB,
) = NARROW = tuple(range(11, 26))
VECTORS = NARROW[:13]
WHOLE = (
    SELF_Q, SELF_QB, SELF_K, SELF_V, SELF_VB, SELF_O,
    SELF_OB, BUCKET_W, BUCKET_B, CROSS_Q, CROSS_QB, CROSS_K,
    CROSS_V, CROSS_VB, CROSS_O, CROSS_OB, FFN_IN, FFN_INB,
    FFN_OUT, FFN_OUTB, GAIN_A, SHIFT_A, GAIN_B, SHIFT_B,
    GAIN_C, SHIFT_C,
)
(
    QUERY, KEYS, VALUES, MIXED, FIRST_LOW, PROBE,
    JOINED, SECOND_LOW, INDEX, CONTENT, SUM_FIRST, SUM_SECOND,
    SUM_THIRD, SLOPE, ACTIVITY, SELF_P, CROSS_P, VECTOR,
) = SAVED = tuple(range(18))


RB, EB, CB = 18, 19, 20
SUM_ORDER = (
    FFN_OUT, FFN_IN, CROSS_O, CROSS_Q, CROSS_V, CROSS_K, SELF_O, SELF_V, SELF_K, SELF_Q, BUCKET_W,
)
POOL = 32
ACTIVITIES, SLOPES, COTANGENT, BRANCH_THREE, SECONDS, JOINEDS, PROBES = 0, 4, 8, 9, 13, 17, 18
INDEXES, CONTENTS, FIRSTS = 19, 21, 23
BRANCH_TWO, GRAD_JOINED, GRAD_PROBE, GRAD_INDEX, GRAD_CONTENT, ENCODED = 8, 0, 1, 2, 24, 6
MIXEDS, QUERIES, KEYSES, VALUESES, TOKENS = 9, 10, 17, 18, 19
BRANCH_ONE, GRAD_MIXED, GRAD_QUERY, GRAD_KEYS, GRAD_VALUES, GRAD_RELATIVE = 20, 21, 22, 0, 8, 23
PARTIALS, PARTIAL_OTHER, PARTIAL_DIAGONAL, PARTIAL_NEXT = 25, 29, 30, 31
GATHER_ORDER = (
    SELF_Q, SELF_K, SELF_V, BUCKET_W, SELF_O, CROSS_Q, CROSS_K, CROSS_V,
    FFN_IN, FFN_IN, CROSS_O, FFN_IN, FFN_IN, FFN_OUT, FFN_OUT, FFN_OUT, FFN_OUT,
)
GROUP = 4
NEXT, OTHER, DIAGONAL = 1, 2, 3


def chips(dp, fsdp):
    square = fsdp
    return (dp // (CORES * square), square, CORES, fsdp)


def place(sizes):
    far, near, cores, side = sizes
    row = lax.axis_index(AXES[0])
    return (row // (near * cores), lax.rem(row // cores, near), lax.rem(row, cores), lax.axis_index(AXES[1]))


def device_at(sizes, spot):
    z, y, c, x = spot
    return ((z * sizes[1] + y) * sizes[2] + c, x)


def moved(spot, level, digit):
    return spot[:level] + (digit,) + spot[level + 1 :]


def peer_at(sizes, me, level, step):
    if level < GROUP:
        return moved(me, level, lax.rem(me[level] + step, sizes[level]))
    core = lax.rem(me[2] + step // sizes[3], sizes[2])
    return (me[0], me[1], core, lax.rem(me[3] + step % sizes[3], sizes[3]))


def reach(sizes, level):
    return sizes[level] if level < GROUP else sizes[2] * sizes[3]


def number_in_group(sizes, spot):
    return spot[2] * sizes[3] + spot[3]


def enter(sizes, me):
    barrier = pltpu.get_barrier_semaphore()
    peers = [(level, step) for level in range(GROUP) for step in range(1, sizes[level])]
    peers += [
        (GROUP, step) for step in range(sizes[3] + 1, sizes[2] * sizes[3]) if step % sizes[3]
    ]
    for level, step in peers:
        pl.semaphore_signal(
            barrier,
            inc=1,
            device_id=device_at(sizes, peer_at(sizes, me, level, step)),
            device_id_type=pl.DeviceIdType.MESH,
        )
    pl.semaphore_wait(barrier, len(peers))


ROUTES = ((0, 1, 3, 2), (0, 3, 1, 2), (3, 1, 0, 2))


def levels_of(which):
    return (0, 1) if which == FFN_OUT else (0, 1, 2, 3)


def gather_route(which, route):
    if which == FFN_OUT:
        return (0, 1)
    return (GROUP, 0, 1) if which == FFN_IN else ROUTES[route]


def sum_route(which, route):
    if which == FFN_OUT:
        return (1, 0)
    return (1, 0, GROUP) if which == FFN_IN else (2,) + ROUTES[route][2::-1]


def without(levels, done):
    gone = tuple(done) + ((2, 3) if GROUP in done else ())
    return tuple(level for level in levels if level not in gone)


def units_of(which, rows, columns):
    if which in (-1, FFN_IN, FFN_OUT) or columns % 256:
        return [(0, rows, 0, columns, 0)]
    half = columns // 2
    return [(0, rows, 0, half, 0), (0, rows, half, half, 1)]


def slots(sizes):
    first = []
    total = 0
    for level in range(GROUP + 1):
        first.append(total)
        total += reach(sizes, level) - 1
    return first, total


def parts_of(devices, which, shape):
    rows, columns = shape[-2:]
    wide = min(columns, WIDE * ROWS // rows)
    if which == FFN_IN:
        wide = WIDE // GROUP
    return (rows, wide), columns // wide


def lane_tile(step, wide):
    if isinstance(step, int):
        return pl.ds(step * wide, wide)
    return pl.ds(pl.multiple_of(step * wide, wide), wide)


def tiles(count, body):
    for step in range(count):
        body(step, 0)


def normal(summed, gain, shift):
    center = summed - jnp.mean(summed, axis=-1, keepdims=True)
    spread = jnp.mean(center * center, axis=-1, keepdims=True)
    return center * lax.rsqrt(spread + 1e-05) * gain + shift


def softmax_rows(scores):
    weights = jnp.exp(scores - jnp.max(scores, axis=-1, keepdims=True))
    return weights * (1.0 / jnp.sum(weights, axis=-1, keepdims=True))


def forward_kernel(sizes, chunks, saved, *refs):
    far, near, cores, side = sizes
    devices = far * near * cores * side
    count = len(MATRICES)
    rows, enc, buckets, valid, small = refs[:5]
    shards, refs = refs[5 : 5 + count], refs[5 + count :]
    outputs, refs = refs[0], refs[1:]
    whole, refs = refs[:count], refs[count:]
    kept, refs = refs[: len(saved)], refs[len(saved) :]
    held = dict(zip(saved, refs[: len(saved)]))
    refs = refs[len(saved) :]
    here, refs = refs[:count], refs[count:]
    vectors, relative, hidden, first, second, wide_bias, partial_out, partial_in, room = refs[:9]
    kept_sem, whole_sem, pair_send, pair_recv, own_sem, send_sem, recv_sem = refs[9:]
    vector = held[VECTOR]
    me = place(sizes)
    slot_of, unused = slots(sizes)
    total = len(chunks)
    units = []
    units_in = []
    for number, (which, part, tall, wide) in enumerate(chunks):
        block_rows = small.shape[0] if which < 0 else whole[which].shape[-2]
        own_units = [(number,) + unit for unit in units_of(which, block_rows, wide)]
        units_in.append(range(len(units), len(units) + len(own_units)))
        units += own_units

    def region(unit, spot, done):
        number, row, tall_rows, column, columns, route = units[unit]
        which, part, tall, wide = chunks[number]
        stay = without(levels_of(which), done)
        index = tuple(
            spot[level] if level in stay else slice(None) for level in levels_of(which)
        )
        if which < 0:
            return vectors.at[index]
        return here[which].at[(part,) + index + (pl.ds(row, tall_rows), pl.ds(column, columns))]

    def own(unit, spot):
        number, row, tall_rows, column, columns, route = units[unit]
        which, part, tall, wide = chunks[number]
        if which < 0:
            return small
        shard = shards[which]
        if which == FFN_IN:
            shard = shard.at[number_in_group(sizes, spot)]
        return shard.at[pl.ds(row, tall_rows), pl.ds(part * wide + column, columns)]

    def route_of(unit):
        return gather_route(chunks[units[unit][0]][0], units[unit][-1])

    def copy(unit, stage, step, from_peer):
        order = route_of(unit)
        level = order[stage]
        size = reach(sizes, level)
        done = order[:stage]
        slot = slot_of[level] + step - 1
        if from_peer:
            peer = peer_at(sizes, me, level, step if level == GROUP else size - step)
            target = region(unit, peer, done)
            source = target
        else:
            peer = peer_at(sizes, me, level, step)
            target = region(unit, me, done)
            source = own(unit, peer) if level == GROUP else target
        return pltpu.make_async_remote_copy(
            src_ref=source,
            dst_ref=target,
            send_sem=send_sem.at[unit, slot],
            recv_sem=recv_sem.at[unit, slot],
            device_id=device_at(sizes, peer),
            device_id_type=pl.DeviceIdType.MESH,
        )

    def steps(unit, stage):
        order = route_of(unit)
        return range(1, reach(sizes, order[stage])) if stage < len(order) else ()

    def keep(unit):
        return pltpu.make_async_copy(own(unit, me), region(unit, me, ()), own_sem.at[unit])

    def start(number, stage):
        for unit in units_in[number]:
            if stage == 0:
                keep(unit).wait()
            for step in steps(unit, stage):
                copy(unit, stage, step, False).start()

    def pass_on(number, stage):
        for unit in units_in[number]:
            for step in steps(unit, stage):
                copy(unit, stage, step, True).wait_recv()
            if stage < 3:
                for step in steps(unit, stage + 1):
                    copy(unit, stage + 1, step, False).start()

    def turn(now):
        if now + AHEAD < total:
            start(now + AHEAD, 0)
        for stage in range(4):
            number = now - LAG * stage
            if 0 <= number < total:
                pass_on(number, stage)

    def write(number):
        which, part, tall, wide = chunks[number]
        return pltpu.make_async_copy(
            here[which].at[part], whole[which].at[part], whole_sem.at[number]
        )

    def weight(number, step=None, tile=256):
        which, part, tall, wide = chunks[number]
        if step is None:
            return here[which][part].reshape(-1, wide)
        return here[which][part, :, :, :, :, :, lane_tile(step, tile)].reshape(-1, tile)

    def row_of(name):
        return NARROW.index(name)

    def project(number, left, into, bias=None, plus=None):
        wide = chunks[number][3]

        def body(step, carry):
            columns = lane_tile(step, 256)
            result = product(left[...], weight(number, step))
            if bias is not None:
                result = result + vector[pl.ds(row_of(bias), 1), columns]
            if plus is not None:
                result = result + plus[:, columns].astype(jnp.float32)
            into[:, columns] = result.astype(into.dtype)
            return carry

        tiles(wide // 256, body)

    def save(*names):
        for name in names:
            number = saved.index(name)
            pltpu.make_async_copy(held[name], kept[number], kept_sem.at[number]).start()

    def norm(summed, gain, shift, into, low):
        def body(step, carry):
            lines = pl.ds(pl.multiple_of(step * 64, 64), 64)
            result = normal(
                summed[lines, :],
                vector[pl.ds(row_of(gain), 1), :],
                vector[pl.ds(row_of(shift), 1), :],
            )
            if into is not None:
                into[lines, :] = result
                low[lines, :] = result.astype(low.dtype)
            else:
                low[lines, :] = (result * valid[lines, :]).astype(low.dtype)
            return carry

        lax.fori_loop(0, summed.shape[0] // 64, body, 0)

    def unpack():
        spots = []
        for index in range(devices):
            x = index % side
            c = index // side % cores
            y = index // (side * cores) % near
            spots.append((index // (side * cores * near), y, c, x))
        blocks = [vectors[spot].astype(jnp.float32) for spot in spots]

        def joined(number, fits):
            return sum(blocks[number * fits + 1 : (number + 1) * fits], blocks[number * fits])

        fits = devices * 128 // vector.shape[1]
        for number in range(devices // fits):
            vector[:, pl.ds(128 * number, 128)] = joined(number, fits)
        row = row_of(BUCKET_B)
        fits = devices * 128 // relative.shape[1]
        for number in range(devices // fits):
            vector[pl.ds(row, 1), pl.ds(128 * number, 128)] = joined(number, fits)[row : row + 1]
        row = row_of(FFN_INB)
        for number in range(far * near):
            spot = (number // near, number % near, me[2], me[3])
            wide_bias[:, pl.ds(128 * number, 128)] = vectors[spot].astype(jnp.float32)[row : row + 1]
        hidden[...] = jnp.where(visible(hidden.shape[0] // 2), 0.0, -1e30)

    def heads(low, high, query, keys, values, probs, mixed, biased):
        lane = lax.broadcasted_iota(jnp.int32, (1, 2 * HEAD_DIM), 1)

        def body(pair, carry):
            columns = lane_tile(pair, 2 * HEAD_DIM)
            one, key, value = query[:, columns], keys[:, columns], values[:, columns]
            reach = keys.shape[0]
            for half in range(2):
                mine = lane // HEAD_DIM == half
                room[half, :, pl.ds(0, reach)] = product_right(
                    jnp.where(mine, one, 0).astype(one.dtype), key
                )
            for half in range(2):
                for line in range(0, one.shape[0], LINES):
                    lines = pl.ds(line, LINES)
                    scores = room[half, lines, pl.ds(0, reach)] * 0.125
                    if biased:
                        fit = 128 // BUCKETS
                        table = relative[lines, lane_tile(pair * 2 // fit, 128)]
                        offset = lax.rem(pair * 2, fit) * BUCKETS + half * BUCKETS
                        found = [
                            jnp.take_along_axis(
                                table, buckets[lines, pl.ds(at, 128)] + offset, axis=1
                            )
                            for at in range(0, reach, 128)
                        ]
                        scores = scores + jnp.concatenate(found, axis=1) + hidden[lines, :]
                    probs[pair, lines, pl.ds(half * reach, reach)] = softmax_rows(scores).astype(
                        jnp.bfloat16
                    )
            results = [
                product(probs[pair, :, pl.ds(half * reach, reach)], value) for half in range(2)
            ]
            mixed[:, columns] = jnp.where(lane < HEAD_DIM, *results).astype(mixed.dtype)
            return carry

        lax.fori_loop(low, high, body, 0)

    def self_heads(low, high):
        heads(
            low, high, held[QUERY], held[KEYS], held[VALUES], held[SELF_P], held[MIXED], True
        )

    def cross_heads(low, high):
        heads(
            low, high, held[PROBE], held[INDEX], held[CONTENT], held[CROSS_P], held[JOINED], False
        )

    def to_item(item, source, target, number):
        return pltpu.make_async_remote_copy(
            src_ref=source,
            dst_ref=target,
            send_sem=pair_send.at[number],
            recv_sem=pair_recv.at[number],
            device_id=device_at(sizes, peer_at(sizes, me, GROUP, item)),
            device_id_type=pl.DeviceIdType.MESH,
        )

    lows = held[SECOND_LOW]

    def share(item):
        if item == DIAGONAL:
            return to_item(OTHER, lows.at[NEXT], lows.at[DIAGONAL], DIAGONAL)
        return to_item(item, lows.at[0], lows.at[item], item)

    def partial(kind, part):
        return to_item(
            NEXT if kind == 2 else OTHER,
            partial_out.at[kind, part],
            partial_in.at[kind, part],
            GROUP + 3 * part + kind,
        )

    amount, width = rows.shape
    def feed(number, item):
        part, tall, wide = chunks[number][1:]
        columns = pl.ds(part * wide, wide)
        room[0, :, pl.ds(0, wide)] = product(lows[item], weight(number))

        def body(step, carry):
            for line in range(2):
                lines = pl.ds(pl.multiple_of(step * 64 + line * 32, 32), 32)
                before = room[0, lines, pl.ds(0, wide)] + wide_bias[:, columns]
                error = 1.0 + lax.erf(before * (0.5**0.5))
                held[ACTIVITY][item, lines, columns] = (0.5 * before * error).astype(jnp.bfloat16)
                slope = 0.5 * error + before * jnp.exp(-0.5 * before * before) * (
                    0.3989422804014327
                )
                held[SLOPE][item, lines, columns] = slope.astype(jnp.bfloat16)
            return carry

        lax.fori_loop(0, amount // 64, body, 0)

    def back(number):
        part, tall, wide = chunks[number][1:]
        columns = pl.ds(part * wide, wide)
        activity = held[ACTIVITY]
        partial_out[0, part] = product(activity[OTHER], weight(number)).astype(jnp.bfloat16)
        partial(0, part).start()
        partial_out[1, part] = product(activity[DIAGONAL], weight(number)).astype(jnp.bfloat16)
        partial(1, part).start()
        first[:, columns] = product(activity[NEXT], weight(number))
        held[SUM_THIRD][:, columns] = (
            product(activity[0], weight(number))
            + vector[pl.ds(row_of(FFN_OUTB), 1), columns]
            + second[:, columns]
        )

    def relay(part):
        wide = width // GROUP
        partial(1, part).wait_recv()
        total_of = first[:, pl.ds(part * wide, wide)] + partial_in[1, part].astype(jnp.float32)
        partial_out[2, part] = total_of.astype(jnp.bfloat16)
        partial(2, part).start()

    pairs = held[QUERY].shape[1] // (2 * HEAD_DIM)

    def compute(number):
        which, part, tall, wide = chunks[number]
        if which < 0:
            unpack()
            save(VECTOR)
            return
        write(number).start()
        name = MATRICES[which]
        if name == SELF_Q:
            project(number, rows, held[QUERY], SELF_QB)
            save(QUERY)
        elif name == SELF_K:
            project(number, rows, held[KEYS])
            save(KEYS)
        elif name == SELF_V:
            project(number, rows, held[VALUES], SELF_VB)
            save(VALUES)
        elif name == BUCKET_W:
            project(number, rows, relative, BUCKET_B)
            self_heads(0, pairs // 2)
        elif name == SELF_O:
            self_heads(pairs // 2, pairs)
            save(SELF_P, MIXED)
            project(number, held[MIXED], held[SUM_FIRST], SELF_OB, rows)
            save(SUM_FIRST)
            norm(held[SUM_FIRST], GAIN_A, SHIFT_A, first, held[FIRST_LOW])
            save(FIRST_LOW)
        elif name == CROSS_K:
            project(number, enc, held[INDEX])
            save(INDEX)
        elif name == CROSS_V:
            project(number, enc, held[CONTENT], CROSS_VB)
            save(CONTENT)
            cross_heads(0, pairs // 2)
        elif name == CROSS_Q:
            project(number, held[FIRST_LOW], held[PROBE], CROSS_QB)
            save(PROBE)
        elif name == CROSS_O:
            cross_heads(pairs // 2, pairs)
            save(CROSS_P, JOINED)
            project(number, held[JOINED], held[SUM_SECOND], CROSS_OB, first)
            save(SUM_SECOND)
            norm(held[SUM_SECOND], GAIN_B, SHIFT_B, second, lows.at[0])
            share(NEXT).start()
            share(OTHER).start()
            feed(number - 2, 0)
            feed(number - 1, 0)
        elif name == FFN_IN and part >= 2:
            feed(number, 0)
            if part == 2:
                share(OTHER).wait_recv()
                for earlier in (number - 3, number - 2):
                    feed(earlier, OTHER)
                share(NEXT).wait_recv()
                share(DIAGONAL).start()
                for earlier in (number - 3, number - 2):
                    feed(earlier, NEXT)
                share(DIAGONAL).wait_recv()
                for earlier in (number - 3, number - 2):
                    feed(earlier, DIAGONAL)
                save(SECOND_LOW)
            for item in (OTHER, NEXT, DIAGONAL):
                feed(number, item)
            if part == 3:
                save(SLOPE, ACTIVITY)
        elif name == FFN_OUT:
            back(number)
            if part > 0:
                relay(part - 1)

    for unit in range(len(units)):
        keep(unit).start()
    enter(sizes, me)
    for number in range(min(AHEAD, total)):
        start(number, 0)
    for now in range(total + 3 * LAG):
        turn(now)
        if now >= 3 * LAG:
            compute(now - 3 * LAG)
    relay(GROUP - 1)
    wide = width // GROUP
    for part in range(GROUP):
        partial(0, part).wait_recv()
        partial(2, part).wait_recv()
        held[SUM_THIRD][:, pl.ds(part * wide, wide)] += partial_in[0, part].astype(
            jnp.float32
        ) + partial_in[2, part].astype(jnp.float32)
    save(SUM_THIRD)
    norm(held[SUM_THIRD], GAIN_C, SHIFT_C, None, outputs)
    for unit in range(len(units)):
        for stage in range(4):
            for step in steps(unit, stage):
                copy(unit, stage, step, False).wait_send()
    for item in (NEXT, OTHER, DIAGONAL):
        share(item).wait_send()
    for part in range(GROUP):
        for kind in range(3):
            partial(kind, part).wait_send()
    for number in range(1, total):
        write(number).wait()
    for number, name in enumerate(saved):
        pltpu.make_async_copy(held[name], kept[number], kept_sem.at[number]).wait()


def forward_all(sizes, small, blocks, rows, enc, buckets, valid):
    devices = sizes[0] * sizes[1] * sizes[2] * sizes[3]
    chunks = [(-1, 0, False, 128)]
    shapes = []
    units = 1
    for which, block in enumerate(blocks):
        part, parts = parts_of(devices, which, block.shape)
        shape = tuple(sizes[level] for level in levels_of(which))
        shapes.append(jax.ShapeDtypeStruct((parts,) + shape + part, block.dtype))
    done = dict.fromkeys(MATRICES, 0)
    for which in GATHER_ORDER:
        part = shapes[which].shape[-2:]
        units += len(units_of(which, *part))
        chunks.append((which, done[which], part[0] > ROWS, part[1]))
        done[which] += 1
    amount, width = rows.shape
    source = enc.shape[0]
    hidden_units = blocks[MATRICES.index(FFN_IN)].shape[-1]
    buckets_wide = blocks[MATRICES.index(BUCKET_W)].shape[1]
    head_count = width // HEAD_DIM
    low, full = jnp.bfloat16, jnp.float32
    one, two = (amount, width), (source, width)
    saved = {
        QUERY: (one, low), KEYS: (one, low), VALUES: (one, low), MIXED: (one, low),
        FIRST_LOW: (one, low), PROBE: (one, low), JOINED: (one, low),
        SECOND_LOW: ((GROUP,) + one, low), INDEX: (two, low), CONTENT: (two, low),
        SUM_FIRST: (one, full), SUM_SECOND: (one, full), SUM_THIRD: (one, full),
        SLOPE: ((GROUP, amount, hidden_units), low), ACTIVITY: ((GROUP, amount, hidden_units), low),
        SELF_P: ((head_count // 2, amount, 2 * amount), low),
        CROSS_P: ((head_count // 2, amount, 2 * source), low),
        VECTOR: ((16, width), full),
    }
    names = SAVED
    unused, places = slots(sizes)
    any_spec = pl.BlockSpec(memory_space=pl.ANY)
    vmem_spec = pl.BlockSpec(memory_space=pltpu.VMEM)
    held = [pltpu.VMEM(*saved[name]) for name in names]
    results = pl.pallas_call(
        partial(forward_kernel, sizes, chunks, names),
        out_shape=[jax.ShapeDtypeStruct(one, low)]
        + shapes
        + [jax.ShapeDtypeStruct(*saved[name]) for name in names],
        in_specs=[vmem_spec] * 4 + [any_spec] * (1 + len(blocks)),
        out_specs=[vmem_spec] + [any_spec] * (len(shapes) + len(names)),
        scratch_shapes=held
        + [pltpu.VMEM(entry.shape, entry.dtype) for entry in shapes]
        + [
            pltpu.VMEM(sizes + small.shape, low),
            pltpu.VMEM((amount, buckets_wide), full),
            pltpu.VMEM((amount, amount), full),
            pltpu.VMEM(one, full),
            pltpu.VMEM(one, full),
            pltpu.VMEM((1, hidden_units), full),
            pltpu.VMEM((3, GROUP, amount, width // GROUP), low),
            pltpu.VMEM((3, GROUP, amount, width // GROUP), low),
            pltpu.VMEM((2, amount, max(amount, source)), full),
            pltpu.SemaphoreType.DMA((len(names),)),
            pltpu.SemaphoreType.DMA((len(chunks),)),
            pltpu.SemaphoreType.DMA((4 * GROUP,)),
            pltpu.SemaphoreType.DMA((4 * GROUP,)),
            pltpu.SemaphoreType.DMA((units,)),
            pltpu.SemaphoreType.DMA((units, places)),
            pltpu.SemaphoreType.DMA((units, places)),
        ],
        compiler_params=pltpu.CompilerParams(
            collective_id=0, has_side_effects=True, vmem_limit_bytes=63 * 1024 * 1024
        ),
        cost_estimate=pl.CostEstimate(flops=10**10, bytes_accessed=1 << 27, transcendentals=10**7),
        name="forward_all",
    )(rows, enc, buckets, valid, small, *blocks)
    whole = dict(zip(MATRICES, results[1 : 1 + len(blocks)]))
    return results[0], whole, dict(zip(names, results[1 + len(blocks) :]))


def backward_kernel(sizes, chunks, flat_room, *refs):
    far, near, cores, side = sizes
    devices = far * near * cores * side
    count = len(MATRICES)
    cotangent, buckets, valid, rows_in, enc_in = refs[:5]
    kept, refs = refs[5 : 5 + len(SAVED)], refs[5 + len(SAVED) :]
    whole, refs = refs[:count], refs[count:]
    small_out, shares, refs = refs[0], refs[1 : 1 + count], refs[1 + count :]
    tokens_out, encoded_out, refs = refs[0], refs[1], refs[2:]
    pool, full, acc, vector, sums, wide_sums, small, relative, picked, room, steep = refs[:11]
    low_slot, tall_slot, self_probs, cross_probs, flat_ring, tall_ring, flat_in = refs[11:18]
    refs = refs[18:]
    total = len(chunks) + 1
    units = []
    units_in = []
    inbox = []
    flats = []
    for number in range(total):
        if number < total - 1:
            which, tall_rows, tall, wide, column = chunks[number]
            own_units = units_of(which, tall_rows, wide)
            if which not in (FFN_IN, FFN_OUT):
                flats.append(number)
        else:
            which = -1
            own_units = units_of(which, *small.shape[4:])
        units_in.append(range(len(units), len(units) + len(own_units)))
        for unit in own_units:
            units.append((number,) + unit)
            if flats and flats[-1] == number:
                shelf = flat_in.at[pl.ds((len(flats) - 1) % flat_room, 1)]
                shelf = shelf.at[:, :, :, :, :, pl.ds(unit[2], unit[3])]
                inbox.append((shelf,) + tuple(refs[:3]))
                refs = refs[3:]
            else:
                deep = len(sum_route(which, 0))
                inbox.append(tuple(refs[:deep]))
                refs = refs[deep:]
    load_sem, slot_sem, self_sem, cross_sem, out_sem, credit = refs[:6]
    pair_send, pair_recv, send_sem, recv_sem = refs[6:]
    me = place(sizes)
    first, unused = slots(sizes)
    z, y, c, x = me
    amount, width = rows_in.shape
    source = enc_in.shape[0]
    pairs = width // (2 * HEAD_DIM)
    slab = width // far

    def loading(which, number, height=1):
        array = {RB: rows_in, EB: enc_in, CB: cotangent}.get(which)
        array = kept[which] if array is None else array
        if which in (SUM_FIRST, SUM_SECOND, SUM_THIRD):
            return [(array, full.at[number], which)]
        if which == VECTOR:
            return [(array, vector, which)]
        if height == 1:
            return [(array, pool.at[number], which)]
        if len(array.shape) == 3:
            return [
                (
                    array.at[part],
                    pool.at[number + part],
                    which,
                )
                for part in range(height)
            ]
        return [
            (array.at[pl.ds(part * amount, amount)], pool.at[number + part], which)
            for part in range(height)
        ]

    semaphores = {}
    waiting = {}

    def fetch(which, number, height=1):
        waiting[which] = []
        for source_ref, target, unused_name in loading(which, number, height):
            semaphores[which, len(waiting[which])] = len(semaphores)
            one = pltpu.make_async_copy(source_ref, target, load_sem.at[len(semaphores) - 1])
            one.start()
            waiting[which].append(one)

    def ready(*names):
        for which in names:
            for one in waiting.pop(which):
                one.wait()

    order = [FFN_IN, CROSS_O, CROSS_Q, SELF_O, CROSS_K, CROSS_V, SELF_Q, SELF_K, SELF_V, BUCKET_W]

    def weight_copies(number):
        which = order[number]
        parts, wide = whole[which].shape[0], whole[which].shape[-1]
        return [
            pltpu.make_async_copy(
                whole[which].at[part],
                low_slot.at[number % 2, :, :, :, :, :, pl.ds(part * wide, wide)],
                slot_sem.at[number % 2 * GROUP + part],
            )
            for part in range(parts)
        ]

    def weight_fetch(number):
        if number < len(order):
            for one in weight_copies(number):
                one.start()

    def weight_ready(number):
        for one in weight_copies(number):
            one.wait()

    def tall_copy():
        return pltpu.make_async_copy(whole[FFN_OUT], tall_slot, slot_sem.at[2 * GROUP])

    def row_of(name):
        return NARROW.index(name)

    def through(which, left, into, fresh=False):
        number = order.index(which)
        wide = whole[which].shape[0] * whole[which].shape[-1]

        def body(step, carry):
            columns = lane_tile(step, slab)
            piece = low_slot[number % 2, step, :, :, :, :, pl.ds(0, wide)].reshape(slab, wide)
            result = product_right(left(), piece)
            if fresh:
                into[:, columns] = result.astype(into.dtype)
            else:
                into[:, columns] += result
            return carry

        tiles(far, body)

    def back_through(which, left, into, fresh=False):
        weight_ready(order.index(which))
        through(which, left, into, fresh)
        weight_fetch(order.index(which) + 2)

    def norm_backward(summed, gain, shift, bias, low, first_grad):
        def body(step, carry):
            lines = pl.ds(pl.multiple_of(step * 64, 64), 64)
            center = summed[lines, :]
            center = center - jnp.mean(center, axis=-1, keepdims=True)
            scale = lax.rsqrt(jnp.mean(center * center, axis=-1, keepdims=True) + 1e-05)
            unit = center * scale
            if first_grad is not None:
                grad = first_grad[lines, :].astype(jnp.float32) * valid[lines, :]
            else:
                grad = acc[lines, :]
            inner = grad * vector[pl.ds(row_of(gain), 1), :]
            inner = inner - jnp.mean(inner, axis=-1, keepdims=True) - unit * jnp.mean(
                inner * unit, axis=-1, keepdims=True
            )
            inner = inner * scale
            branch = inner.astype(jnp.bfloat16)
            acc[lines, :] = inner
            low[lines, :] = branch
            sums[pl.ds(row_of(gain), 1), :] += jnp.sum(grad * unit, axis=0, keepdims=True)
            sums[pl.ds(row_of(shift), 1), :] += jnp.sum(grad, axis=0, keepdims=True)
            sums[pl.ds(row_of(bias), 1), :] += jnp.sum(
                branch.astype(jnp.float32), axis=0, keepdims=True
            )
            return carry

        lax.fori_loop(0, amount // 64, body, 0)

    def feed_backward(item):
        parts, wide = whole[FFN_OUT].shape[0], whole[FFN_OUT].shape[-1]
        tile = near * chunks[0][1]

        def body(step, carry):
            columns = lane_tile(step, tile)
            grad = 0.0
            for part in range(parts):
                piece = tall_slot[part, step].reshape(tile, wide)
                left = pool[BRANCH_THREE + item, :, pl.ds(part * wide, wide)]
                grad = grad + product_right(left, piece)
            slope = pool[SLOPES + item, :, columns].astype(jnp.float32)
            grad = (grad * slope).astype(jnp.bfloat16)
            pool[SLOPES + item, :, columns] = grad
            wide_sums[:, columns] += jnp.sum(grad.astype(jnp.float32), axis=0, keepdims=True)
            return carry

        tiles(far, body)

    def probs_copy(which, pair, slot):
        buffer, sem = (cross_probs, cross_sem) if which == CROSS_P else (self_probs, self_sem)
        return pltpu.make_async_copy(kept[which].at[pair], buffer.at[slot], sem.at[slot])

    def heads_backward(which, low, high, places, tall):
        query, keys, values, grad_out, to_query, to_keys, to_values = places
        buffer = cross_probs if which == CROSS_P else self_probs
        lane = lax.broadcasted_iota(jnp.int32, (1, 2 * HEAD_DIM), 1)
        span = tall * amount

        def body(pair, carry):
            columns = lane_tile(pair, 2 * HEAD_DIM)
            slot = lax.rem(pair, 2)
            probs_copy(which, pair, slot).wait()

            @pl.when(pair + 1 < pairs)
            def _():
                probs_copy(which, pair + 1, 1 - slot).start()

            one = pool[query, :, columns]
            grad = pool[grad_out, :, columns]
            key = pool[pl.ds(keys, tall), :, columns].reshape(span, 2 * HEAD_DIM)
            value = pool[pl.ds(values, tall), :, columns].reshape(span, 2 * HEAD_DIM)
            found = []
            for half in range(2):
                mine = lane // HEAD_DIM == half
                room[half, :, pl.ds(0, span)] = product_right(
                    jnp.where(mine, grad, 0).astype(grad.dtype), value
                )
            for half in range(2):
                for line in range(0, amount, LINES):
                    lines = pl.ds(line, LINES)
                    prob = buffer[slot, lines, pl.ds(half * span, span)].astype(jnp.float32)
                    weighted = prob * room[half, lines, pl.ds(0, span)]
                    scores = weighted - prob * jnp.sum(weighted, axis=-1, keepdims=True)
                    scores = scores.astype(jnp.bfloat16)
                    steep[half, lines, pl.ds(0, span)] = scores
                    if which == SELF_P:
                        picked[half, lines, :] = scores[:, :target].astype(jnp.float32)
                if which == SELF_P:
                    gather_buckets(pair, half)
            for half in range(2):
                scores = steep[half, :, pl.ds(0, span)]
                prob = buffer[slot, :, pl.ds(half * span, span)]
                found.append(
                    (
                        product(scores, key) * 0.125,
                        product_left(scores, one) * 0.125,
                        product_left(prob, grad),
                    )
                )
            if which == SELF_P:
                spread_buckets(pair)
            merged = [
                jnp.where(lane < HEAD_DIM, left, right).astype(jnp.bfloat16)
                for left, right in zip(*found)
            ]
            pool[to_query, :, columns] = merged[0]
            pool[pl.ds(to_keys, tall), :, columns] = merged[1].reshape(tall, amount, 2 * HEAD_DIM)
            pool[pl.ds(to_values, tall), :, columns] = merged[2].reshape(tall, amount, 2 * HEAD_DIM)
            biases = (SELF_QB, SELF_VB) if which == SELF_P else (CROSS_QB, CROSS_VB)
            for bias, grads in zip(biases, (merged[0], merged[2])):
                sums[pl.ds(row_of(bias), 1), columns] = jnp.sum(
                    grads.astype(jnp.float32), axis=0, keepdims=True
                )
            return carry

        lax.fori_loop(low, high, body, 0)

    target = amount // 2
    fit = 128 // BUCKETS

    def gather_buckets(pair, half):
        own = steep[half, pl.ds(target, target), pl.ds(target, target)].astype(jnp.float32)
        own = jnp.sum(own, axis=1, keepdims=True)
        line = lax.broadcasted_iota(jnp.int32, (target, target), 0)
        lane = lax.broadcasted_iota(jnp.int32, (target, target), 1)
        bucket = jnp.sum(
            jnp.where(line == lane, buckets[target:, target:], 0).astype(jnp.float32),
            axis=1,
            keepdims=True,
        ).astype(jnp.int32)
        offset = lax.rem(pair * 2, fit) * BUCKETS + half * BUCKETS
        block = lane_tile(pair * 2 // fit, 128)
        relative[pl.ds(target, target), block] += jnp.where(lane == bucket + offset, own, 0.0)

    def spread_buckets(pair):
        block = lane_tile(pair * 2 // fit, 128)
        some = 8
        line = lax.broadcasted_iota(jnp.int32, (some * target, 128), 0)
        lane = lax.broadcasted_iota(jnp.int32, (some * target, 128), 1)

        def body(step, carry):
            for half in range(2):
                offset = lax.rem(pair * 2, fit) * BUCKETS + half * BUCKETS
                held = [
                    jnp.where(
                        buckets[:, :target] == some * step + other, picked[half], 0.0
                    ).astype(jnp.bfloat16)
                    for other in range(some)
                ]
                chosen = lane == offset + some * step + line // target
                relative[:, block] += product(
                    jnp.concatenate(held, axis=1), jnp.where(chosen, 1.0, 0.0).astype(jnp.bfloat16)
                )
            return carry

        lax.fori_loop(0, BUCKETS // some, body, 0)

    def held(number):
        if number == total - 1:
            return small, None
        tall, wide = chunks[number][2:4]
        same = [other for other in range(number) if chunks[other][2] == tall]
        ring = tall_ring if tall else flat_ring
        size = ring.shape[0]
        ref = ring.at[len(same) % size]
        if not tall:
            ref = ref.at[:, :, :, :, :, pl.ds(0, wide)]
        return ref, same[-size] if len(same) >= size else None

    def stage_of(unit, stage):
        number, row, tall_rows, column, columns, route = units[unit]
        which = chunks[number][0] if number < total - 1 else -1
        order_of = sum_route(which, route)
        before = without(levels_of(which), order_of[:stage])
        if stage == 0:
            from_ref = held(number)[0]
            if number < total - 1:
                every = (slice(None),) * len(levels_of(which))
                from_ref = from_ref.at[every + (pl.ds(row, tall_rows), pl.ds(column, columns))]
        else:
            from_ref = inbox[unit][stage - 1].at[0]
        return from_ref, before, order_of[stage], inbox[unit][stage]

    def pick(ref, levels, level, spot, step=None):
        index = []
        for other in levels:
            if other == level or (level == GROUP and other in (2, 3)):
                index.append(spot[other])
            elif other == 0 and step is not None:
                index.append(step)
            else:
                index.append(slice(None))
        return ref.at[tuple(index)] if index else ref

    def stages(unit):
        number = units[unit][0]
        return len(sum_route(chunks[number][0] if number < total - 1 else -1, 0))

    def copies(unit, stage):
        if stage >= stages(unit):
            return []
        from_ref, before, level, into = stage_of(unit, stage)
        found = []
        for step in range(1, reach(sizes, level)):
            peer = peer_at(sizes, me, level, step)
            slot = first[level] + step - 1
            found.append(
                pltpu.make_async_remote_copy(
                    src_ref=pick(from_ref, before, level, peer),
                    dst_ref=into.at[step - 1],
                    send_sem=send_sem.at[unit, slot],
                    recv_sem=recv_sem.at[unit, slot],
                    device_id=device_at(sizes, peer),
                    device_id_type=pl.DeviceIdType.MESH,
                )
            )
        return found

    def start(number):
        if number in flats and flats.index(number) >= flat_room:
            pl.semaphore_wait(credit, cores - 1)
        for unit in units_in[number]:
            for one in copies(unit, 0):
                one.start()

    waited = set()

    def sent(number, stage):
        for unit in units_in[number]:
            if (unit, stage) not in waited:
                waited.add((unit, stage))
                for one in copies(unit, stage):
                    one.wait_send()

    def add(unit, stage):
        if stage >= stages(unit):
            return
        from_ref, before, level, into = stage_of(unit, stage)
        after = without(before, (level,))
        number, row, tall_rows, column, columns, route = units[unit]
        last = stage == stages(unit) - 1
        if last and number < total - 1 and chunks[number][0] == FFN_IN:
            spot = (pl.ds(row, tall_rows), pl.ds(chunks[number][4] + column, columns))
            shares[FFN_IN][(number_in_group(sizes, me),) + spot] = from_ref[c, x].astype(jnp.float32)
            for step in range(1, reach(sizes, GROUP)):
                peer = peer_at(sizes, me, GROUP, step)
                shares[FFN_IN][(number_in_group(sizes, peer),) + spot] = into[step - 1].astype(
                    jnp.float32
                )
            return

        def one(step):
            here = pick(from_ref, before, level, me, step)[...]
            if last:
                here = here.astype(jnp.float32)
            for other in range(1, reach(sizes, level)):
                here = here + pick(into.at[other - 1], after, None, None, step)[...]
            return here

        if last:
            if number == total - 1:
                small_out[...] = one(None)
            else:
                which, block_rows, tall, wide, base = chunks[number]
                shares[which][pl.ds(row, tall_rows), pl.ds(base + column, columns)] = one(None)
        elif 0 in after:

            def body(step, carry):
                pick(into.at[0], after, None, None, step)[...] = one(step)
                return carry

            lax.fori_loop(0, far, body, 0)
        else:
            into[0] = one(None)

    def pass_on(number, stage):
        for unit in units_in[number]:
            for one in copies(unit, stage):
                one.wait_recv()
            add(unit, stage)
            if stage < 3:
                for one in copies(unit, stage + 1):
                    one.start()
        if stage == 1 and number in flats and flats.index(number) + flat_room < len(flats):
            sent(number, 1)
            for step in range(1, cores):
                pl.semaphore_signal(
                    credit,
                    inc=1,
                    device_id=device_at(sizes, moved(me, 2, lax.rem(c + step, cores))),
                    device_id_type=pl.DeviceIdType.MESH,
                )

    def produce(number, left, right):
        ref, previous = held(number)
        if previous is not None:
            sent(previous, 0)
        which, tall_rows, tall, wide, column = chunks[number]
        height = near * tall_rows if tall else slab
        right_value = right

        def body(step, carry):
            grad = product_left(left(step, height), right_value()).astype(jnp.bfloat16)
            into = ref.at[step]
            into[...] = grad.reshape(into.shape)
            return carry

        tiles(far, body)

    emitted = {}

    def emit(now, number, left=None, right=None):
        if left is not None:
            produce(number, left, right)
        start(number)
        emitted[number] = now

    def turn(now):
        for stage in (3, 2, 1, 0):
            for number, began in emitted.items():
                if began + 1 + LAG * stage == now:
                    pass_on(number, stage)

    def lanes_of(slot, height=1):
        def part(step, wide):
            if height == 1:
                return pool[slot, :, lane_tile(step, wide)]
            return pool[pl.ds(slot, height), :, lane_tile(step, wide)].reshape(height * amount, wide)

        return part

    def all_of(slot, height=1, wide=None):
        wide = width if wide is None else wide

        def part():
            if height == 1:
                return pool[slot, :, pl.ds(0, wide)]
            return pool[pl.ds(slot, height), :, pl.ds(0, wide)].reshape(height * amount, wide)

        return part

    fetch(SUM_THIRD, 0)
    fetch(CB, COTANGENT)
    fetch(VECTOR, 0)
    tall_copy().start()
    fetch(SLOPE, SLOPES, GROUP)
    weight_fetch(0)
    weight_fetch(1)
    fetch(ACTIVITY, ACTIVITIES, GROUP)
    fetch(SECOND_LOW, SECONDS, GROUP)
    wide_sums[...] = jnp.zeros_like(wide_sums)
    fetch(SUM_SECOND, 1)
    fetch(JOINED, JOINEDS)
    fetch(PROBE, PROBES)
    fetch(INDEX, INDEXES, 2)
    fetch(CONTENT, CONTENTS, 2)
    fetch(FIRST_LOW, FIRSTS)
    probs_copy(CROSS_P, 0, 0).start()
    probs_copy(SELF_P, 0, 0).start()
    sums[...] = jnp.zeros_like(sums)
    relative[...] = jnp.zeros_like(relative)
    enter(sizes, me)

    ready(SUM_THIRD, CB, VECTOR)
    norm_backward(full.at[0], GAIN_C, SHIFT_C, FFN_OUTB, pool.at[BRANCH_THREE], pool.at[COTANGENT])

    def to_item(item, source_slot, target_slot, number):
        return pltpu.make_async_remote_copy(
            src_ref=pool.at[source_slot],
            dst_ref=pool.at[target_slot],
            send_sem=pair_send.at[number],
            recv_sem=pair_recv.at[number],
            device_id=device_at(sizes, peer_at(sizes, me, GROUP, item)),
            device_id_type=pl.DeviceIdType.MESH,
        )

    branch_next = to_item(NEXT, BRANCH_THREE, BRANCH_THREE + NEXT, 0)
    branch_other = to_item(OTHER, BRANCH_THREE, BRANCH_THREE + OTHER, 1)
    branch_diagonal = to_item(OTHER, BRANCH_THREE + NEXT, BRANCH_THREE + DIAGONAL, 2)
    partial_other = to_item(OTHER, PARTIALS + OTHER, PARTIAL_OTHER, 3)
    partial_diagonal = to_item(OTHER, PARTIALS + DIAGONAL, PARTIAL_DIAGONAL, 4)
    partial_next = to_item(NEXT, PARTIALS + NEXT, PARTIAL_NEXT, 5)

    def slab_backward(item):
        feed_backward(item)
        left = all_of(SLOPES + item)
        if item == 0:
            through(FFN_IN, left, acc)
        else:
            through(FFN_IN, left, pool.at[PARTIALS + item], True)

    branch_next.start()
    branch_other.start()
    tall_copy().wait()
    ready(SLOPE)
    weight_ready(0)
    slab_backward(0)
    branch_other.wait()
    slab_backward(OTHER)
    partial_other.start()
    branch_next.wait_recv()
    branch_diagonal.start()
    ready(ACTIVITY, SECOND_LOW)
    fetch(SUM_FIRST, 0)

    def activity_lanes(step, wide):
        columns = lane_tile(step, wide)
        return pool[pl.ds(ACTIVITIES, GROUP), :, columns].reshape(GROUP * amount, wide)

    def third_lanes(part):
        wide = chunks[part][3]
        return lambda: pool[pl.ds(BRANCH_THREE, GROUP), :, pl.ds(part * wide, wide)].reshape(
            GROUP * amount, wide
        )

    def slab_lanes(part):
        wide = chunks[GROUP + part][3]
        return lambda: pool[pl.ds(SLOPES, GROUP), :, pl.ds(part * wide, wide)].reshape(
            GROUP * amount, wide
        )

    cross_places = (PROBES, INDEXES, CONTENTS, GRAD_JOINED, GRAD_PROBE, GRAD_INDEX, GRAD_CONTENT)
    self_places = (QUERIES, KEYSES, VALUESES, GRAD_MIXED, GRAD_QUERY, GRAD_KEYS, GRAD_VALUES)

    def second_backward():
        ready(SUM_SECOND, JOINED, PROBE, INDEX, CONTENT, FIRST_LOW)
        partial_other.wait()
        partial_next.wait()
        acc[...] += pool[PARTIAL_OTHER].astype(jnp.float32) + pool[PARTIAL_NEXT].astype(jnp.float32)
        norm_backward(full.at[1], GAIN_B, SHIFT_B, CROSS_OB, pool.at[BRANCH_TWO], None)
        back_through(CROSS_O, all_of(BRANCH_TWO), pool.at[GRAD_JOINED], True)

    def cross_backward(low):
        heads_backward(CROSS_P, low, low + pairs // 4, cross_places, source // amount)

    def first_backward():
        back_through(CROSS_Q, all_of(GRAD_PROBE), acc)
        ready(SUM_FIRST)
        norm_backward(full.at[0], GAIN_A, SHIFT_A, SELF_OB, pool.at[BRANCH_ONE], None)
        back_through(SELF_O, all_of(BRANCH_ONE), pool.at[GRAD_MIXED], True)

    def self_backward(low):
        if low == 0:
            ready(QUERY, KEYS, VALUES)
        heads_backward(SELF_P, low, low + pairs // 4, self_places, 1)

    step = pairs // 4
    slab_backward(NEXT)
    branch_diagonal.wait_recv()
    emit(0, 0, activity_lanes, third_lanes(0))
    slab_backward(DIAGONAL)
    weight_fetch(2)
    partial_diagonal.start()
    turn(0)
    emit(1, 1, activity_lanes, third_lanes(1))
    partial_diagonal.wait_recv()
    pool[PARTIALS + NEXT] = (
        pool[PARTIALS + NEXT].astype(jnp.float32) + pool[PARTIAL_DIAGONAL].astype(jnp.float32)
    ).astype(jnp.bfloat16)
    partial_next.start()
    for one in (branch_next, branch_diagonal, partial_diagonal):
        one.wait_send()
    turn(1)
    emit(2, 2, activity_lanes, third_lanes(2))
    turn(2)
    emit(3, 3, activity_lanes, third_lanes(3))
    turn(3)
    emit(4, 4, lanes_of(SECONDS, GROUP), slab_lanes(0))
    second_backward()
    turn(4)
    emit(5, 5, lanes_of(SECONDS, GROUP), slab_lanes(1))
    cross_backward(0)
    turn(5)
    emit(6, 6, lanes_of(SECONDS, GROUP), slab_lanes(2))
    cross_backward(step)
    turn(6)
    emit(7, 7, lanes_of(SECONDS, GROUP), slab_lanes(3))
    fetch(EB, ENCODED, 2)
    fetch(QUERY, QUERIES)
    fetch(MIXED, MIXEDS)
    cross_backward(2 * step)
    turn(7)
    emit(8, 8, lanes_of(JOINEDS), all_of(BRANCH_TWO))
    fetch(KEYS, KEYSES)
    cross_backward(3 * step)
    fetch(VALUES, VALUESES)
    fetch(RB, TOKENS)
    turn(8)
    emit(9, 9, lanes_of(FIRSTS), all_of(GRAD_PROBE))
    first_backward()
    turn(9)
    ready(EB)
    emit(10, 10, lanes_of(ENCODED, 2), all_of(GRAD_CONTENT, 2))
    self_backward(0)
    turn(10)
    emit(11, 11, lanes_of(ENCODED, 2), all_of(GRAD_INDEX, 2))
    self_backward(step)
    turn(11)
    ready(MIXED)
    emit(12, 12, lanes_of(MIXEDS), all_of(BRANCH_ONE))
    self_backward(2 * step)
    turn(12)
    self_backward(3 * step)
    ready(RB)
    now = 13
    pool[GRAD_RELATIVE, :, pl.ds(0, relative.shape[1])] = relative[...].astype(jnp.bfloat16)
    sums[pl.ds(row_of(BUCKET_B), 1), pl.ds(0, relative.shape[1])] = jnp.sum(
        relative[...].astype(jnp.bfloat16).astype(jnp.float32), axis=0, keepdims=True
    )
    fits = devices * 128 // width
    for index in range(devices):
        spot = (
            index // (side * cores * near),
            index // (side * cores) % near,
            index // side % cores,
            index % side,
        )
        small[spot] = sums[:, pl.ds(index // fits * 128, 128)]
        block = index * relative.shape[1] // (devices * 128)
        small[spot + (pl.ds(row_of(BUCKET_B), 1),)] = sums[
            pl.ds(row_of(BUCKET_B), 1), pl.ds(block * 128, 128)
        ]
    for index in range(far * near):
        spot = (index // near, index % near, c, x)
        small[spot + (pl.ds(row_of(FFN_INB), 1),)] = wide_sums[:, pl.ds(index * 128, 128)]
    emit(now, 17)
    last = (
        (13, GRAD_VALUES, width),
        (14, GRAD_KEYS, width),
        (15, GRAD_QUERY, width),
        (16, GRAD_RELATIVE, relative.shape[1]),
    )
    for number, grads, wide in last:
        emit(now, number, lanes_of(TOKENS), all_of(grads, 1, wide))
        turn(now)
        now += 1

    def encoded_part(which, slot, fresh):
        number = order.index(which)
        weight_ready(number)

        def body(step, carry):
            columns = lane_tile(step, slab)
            piece = low_slot[number % 2, step].reshape(slab, width)
            result = product_right(all_of(slot, 2)(), piece)
            for part in range(source // amount):
                lines = result[part * amount : (part + 1) * amount]
                if fresh:
                    full[part, :, columns] = lines
                else:
                    full[part, :, columns] += lines
            return carry

        tiles(far, body)
        weight_fetch(number + 2)

    drain = [
        lambda: encoded_part(CROSS_K, GRAD_INDEX, True),
        lambda: encoded_part(CROSS_V, GRAD_CONTENT, False),
        lambda: back_through(SELF_Q, all_of(GRAD_QUERY), acc),
        lambda: back_through(SELF_K, all_of(GRAD_KEYS), acc),
        lambda: back_through(SELF_V, all_of(GRAD_VALUES), acc),
        lambda: back_through(BUCKET_W, all_of(GRAD_RELATIVE, 1, relative.shape[1]), acc),
    ]
    results = [
        pltpu.make_async_copy(
            full.at[part], encoded_out.at[pl.ds(part * amount, amount)], out_sem.at[part]
        )
        for part in range(source // amount)
    ]
    results.append(pltpu.make_async_copy(acc, tokens_out, out_sem.at[len(results)]))
    end = max(emitted.values()) + 1 + 3 * LAG
    piece = 0
    while now <= end or piece < len(drain):
        if piece < len(drain):
            drain[piece]()
            piece += 1
            if piece == 2:
                for one in results[:-1]:
                    one.start()
            if piece == len(drain):
                results[-1].start()
        turn(now)
        now += 1
    for number in range(total):
        for stage in range(4):
            sent(number, stage)
    for one in results:
        one.wait()


def backward_all(sizes, whole, kept, rows, enc, cotangent, buckets, valid):
    devices = sizes[0] * sizes[1] * sizes[2] * sizes[3]
    chunks = []
    for which in SUM_ORDER:
        parts, tall_rows, wide = whole[which].shape[0], whole[which].shape[-2], whole[which].shape[-1]
        for part in range(parts):
            chunks.append((which, tall_rows, tall_rows > ROWS, wide, part * wide))
    flat_room, low, full = 6, jnp.bfloat16, jnp.float32
    amount, width = rows.shape
    wide_rows, tall_wide = whole[FFN_OUT].shape[-2:]
    hidden_units = wide_rows * devices // GROUP
    buckets_wide = whole[BUCKET_W].shape[-1]
    far, near, cores, side = sizes
    inbox = []
    total = 0
    for number in range(len(chunks) + 1):
        summed = number < len(chunks)
        block = (chunks[number][1], chunks[number][3]) if summed else (16, 128)
        kind = low if summed else full
        which = chunks[number][0] if summed else -1
        for row, tall_rows, column, columns, route in units_of(which, *block):
            total += 1
            left = levels_of(which)
            for stage, level in enumerate(sum_route(which, route)):
                left = without(left, (level,))
                if stage > 0 or which in (FFN_IN, FFN_OUT, -1):
                    shape = (reach(sizes, level) - 1,) + tuple(sizes[one] for one in left)
                    inbox.append(pltpu.VMEM(shape + (tall_rows, columns), kind))
    unused, places = slots(sizes)
    any_spec = pl.BlockSpec(memory_space=pl.ANY)
    vmem_spec = pl.BlockSpec(memory_space=pltpu.VMEM)
    shapes = []
    for which in MATRICES:
        shape = (whole[which].shape[-2], whole[which].shape[0] * whole[which].shape[-1])
        if which == FFN_IN:
            shape = (GROUP,) + shape
        shapes.append(jax.ShapeDtypeStruct(shape, full))
    results = pl.pallas_call(
        partial(backward_kernel, sizes, chunks, flat_room),
        out_shape=[jax.ShapeDtypeStruct((16, 128), full)]
        + shapes
        + [jax.ShapeDtypeStruct(rows.shape, full), jax.ShapeDtypeStruct(enc.shape, full)],
        in_specs=[any_spec, vmem_spec, vmem_spec] + [any_spec] * (2 + len(SAVED) + len(MATRICES)),
        out_specs=[vmem_spec] * (1 + len(MATRICES)) + [any_spec] * 2,
        scratch_shapes=[
            pltpu.VMEM((POOL, amount, width), low),
            pltpu.VMEM((2, amount, width), full),
            pltpu.VMEM((amount, width), full),
            pltpu.VMEM((16, width), full),
            pltpu.VMEM((16, width), full),
            pltpu.VMEM((1, hidden_units), full),
            pltpu.VMEM(sizes + (16, 128), full),
            pltpu.VMEM((amount, buckets_wide), full),
            pltpu.VMEM((2, amount, amount // 2), full),
            pltpu.VMEM((2, amount, max(amount, enc.shape[0])), full),
            pltpu.VMEM((2, amount, max(amount, enc.shape[0])), low),
            pltpu.VMEM((2,) + sizes + (ROWS, WIDE), low),
            pltpu.VMEM(whole[FFN_OUT].shape, low),
            pltpu.VMEM((2,) + kept[SELF_P].shape[1:], low),
            pltpu.VMEM((2,) + kept[CROSS_P].shape[1:], low),
            pltpu.VMEM((3,) + sizes + (ROWS, WIDE), low),
            pltpu.VMEM((2, far, near, wide_rows, tall_wide), low),
            pltpu.VMEM((flat_room, far, near, side, ROWS, WIDE), low),
        ]
        + inbox
        + [
            pltpu.SemaphoreType.DMA((32,)),
            pltpu.SemaphoreType.DMA((2 * GROUP + 1,)),
            pltpu.SemaphoreType.DMA((2,)),
            pltpu.SemaphoreType.DMA((2,)),
            pltpu.SemaphoreType.DMA((1 + enc.shape[0] // amount,)),
            pltpu.SemaphoreType.REGULAR,
            pltpu.SemaphoreType.DMA((6,)),
            pltpu.SemaphoreType.DMA((6,)),
            pltpu.SemaphoreType.DMA((total, places)),
            pltpu.SemaphoreType.DMA((total, places)),
        ],
        compiler_params=pltpu.CompilerParams(
            collective_id=1,
            has_side_effects=True,
            vmem_limit_bytes=63 * 1024 * 1024,
            fuse_transposed_lhs_in_matmul=True,
        ),
        cost_estimate=pl.CostEstimate(flops=2 * 10**10, bytes_accessed=1 << 27, transcendentals=0),
        name="backward_all",
    )(
        cotangent,
        buckets,
        valid,
        rows,
        enc,
        *[kept[name] for name in SAVED],
        *[whole[name] for name in MATRICES],
    )
    return results[0], results[1 : 1 + len(MATRICES)], results[-2], results[-1]


def finish_kernel(count, *refs):
    ins, outs, sem = refs[:count], refs[count : 2 * count], refs[2 * count]
    copies = [pltpu.make_async_copy(ins[one], outs[one], sem.at[one]) for one in range(count)]
    for one in copies:
        one.start()
    for one in copies:
        one.wait()


def finish(arrays):
    return pl.pallas_call(
        partial(finish_kernel, len(arrays)),
        out_shape=[jax.ShapeDtypeStruct(array.shape, array.dtype) for array in arrays],
        in_specs=[pl.BlockSpec(memory_space=pl.ANY)] * len(arrays),
        out_specs=[pl.BlockSpec(memory_space=pltpu.VMEM)] * len(arrays),
        scratch_shapes=[pltpu.SemaphoreType.DMA((len(arrays),))],
        name="finish",
    )(*arrays)


def quarters(sizes, block):
    split = block.reshape(block.shape[0], sizes[0] * sizes[1], GROUP, -1)
    return split.transpose(2, 0, 1, 3).reshape(GROUP, block.shape[0], -1)


def own_index():
    return lax.axis_index(AXES[0]) * lax.psum(1, AXES[1]) + lax.axis_index(AXES[1])


def spread_small(params):
    lane = lax.broadcasted_iota(jnp.int32, (1, 128), 1)
    index = own_index()
    rows = []
    for names in (VECTORS,) + tuple((name,) for name in NARROW[len(VECTORS) :]):
        width = params[names[0]].shape[0]
        fits = 128 // width
        block = jnp.tile(jnp.stack([params[name] for name in names]), (1, fits))
        rows.append(jnp.where(lane // width == lax.rem(index, fits), block, 0))
    rows.append(jnp.zeros((16 - len(NARROW), 128), rows[0].dtype))
    return jnp.concatenate(rows)


def deliver(pairs, sums):
    grads = dict(sums)
    for name in MATRICES:
        grads[name] = product_left(*pairs[name])
    return tuple(
        lax.psum_scatter(grads[name], AXES, scatter_dimension=0, tiled=True) for name in WHOLE
    )


def product(left, right):
    return jnp.dot(left, right, preferred_element_type=jnp.float32)


def product_left(left, right):
    return lax.dot_general(
        left, right, (((0,), (0,)), ((), ())), preferred_element_type=jnp.float32
    )


def product_right(left, right):
    return lax.dot_general(
        left, right, (((1,), (1,)), ((), ())), preferred_element_type=jnp.float32
    )


def column_sum(grad):
    return jnp.sum(grad.astype(jnp.float32), axis=0)


def layer_norm(summed, gain, shift):
    center = summed - jnp.mean(summed, axis=-1, keepdims=True)
    spread = jnp.mean(center * center, axis=-1, keepdims=True)
    return center * lax.rsqrt(spread + 1e-05) * gain.astype(jnp.float32) + shift.astype(jnp.float32)


def norm_back(summed, gain, shift, grad):
    unused, pull = jax.vjp(layer_norm, summed, gain.astype(jnp.float32), shift.astype(jnp.float32))
    return pull(grad)


def visible(target):
    place = jnp.arange(2 * target, dtype=jnp.int32) % target
    stream = jnp.arange(2 * target, dtype=jnp.int32) // target
    row_place = place[:, None]
    key_place = place[None, :]
    row_stream = stream[:, None]
    key_stream = stream[None, :]
    earlier = (key_stream == 0) & (
        (row_stream == 0) & (key_place <= row_place) | (row_stream == 1) & (key_place < row_place)
    )
    itself = (key_stream == 1) & (row_stream == 1) & (key_place == row_place)
    return earlier | itself


def valid_rows(lengths, target):
    valid = (jnp.arange(target, dtype=jnp.int32)[None, :] < lengths[:, None]).astype(jnp.float32)
    return jnp.concatenate([valid, valid], axis=1).reshape(-1)


def bucket_table(buckets):
    count, streams, target, width = buckets.shape
    flat = buckets.reshape(count, streams * target, width)
    return (
        flat[:, :, None, :] == jnp.arange(BUCKETS, dtype=jnp.int32)[None, None, :, None]
    ).astype(jnp.float32)


def relative_bias(onehot, relative):
    table = relative.reshape(onehot.shape[0], onehot.shape[1], -1, BUCKETS)
    return jnp.einsum("nqbk,nqhb->nhqk", onehot, table, precision=lax.Precision.HIGHEST)


def scores_of(query, keys, bias, allowed):
    scores = (
        jnp.einsum("nqhd,nkhd->nhqk", query, keys, preferred_element_type=jnp.float32) * 0.125
        + bias
    )
    return jnp.where(allowed, scores, -1e30)


def attend(query, keys, values, bias, allowed):
    scores = scores_of(query, keys, bias, allowed)
    top = jnp.max(scores, axis=-1, keepdims=True)
    logsum = top + jnp.log(jnp.sum(jnp.exp(scores - top), axis=-1, keepdims=True))
    probs = jnp.exp(scores - logsum).astype(jnp.bfloat16)
    mixed = jnp.einsum("nhqk,nkhd->nqhd", probs, values, preferred_element_type=jnp.float32)
    return (mixed.astype(jnp.bfloat16), logsum)


def attend_back(query, keys, values, bias, allowed, logsum, grad_out):
    probs = jnp.exp(scores_of(query, keys, bias, allowed) - logsum)
    grad_probs = jnp.einsum("nqhd,nkhd->nhqk", grad_out, values, preferred_element_type=jnp.float32)
    grad_scores = (
        probs * (grad_probs - jnp.sum(probs * grad_probs, axis=-1, keepdims=True))
    ).astype(jnp.bfloat16)
    grad_query = (
        jnp.einsum("nhqk,nkhd->nqhd", grad_scores, keys, preferred_element_type=jnp.float32) * 0.125
    ).astype(jnp.bfloat16)
    grad_keys = (
        jnp.einsum("nhqk,nqhd->nkhd", grad_scores, query, preferred_element_type=jnp.float32)
        * 0.125
    ).astype(jnp.bfloat16)
    grad_values = jnp.einsum(
        "nhqk,nqhd->nkhd", probs.astype(jnp.bfloat16), grad_out, preferred_element_type=jnp.float32
    ).astype(jnp.bfloat16)
    return (grad_scores, grad_query, grad_keys, grad_values)


def forward(whole, tokens, encoded, buckets):
    (
        self_q,
        self_qb,
        self_k,
        self_v,
        self_vb,
        self_o,
        self_ob,
        bucket_w,
        bucket_b,
        cross_q,
        cross_qb,
        cross_k,
        cross_v,
        cross_vb,
        cross_o,
        cross_ob,
        ffn_in,
        ffn_inb,
        ffn_out,
        ffn_outb,
        gain_a,
        shift_a,
        gain_b,
        shift_b,
        gain_c,
        shift_c,
    ) = whole
    count, streams, target, width = tokens.shape
    source = encoded.shape[1]
    head_shape = (count, streams * target, width // HEAD_DIM, HEAD_DIM)
    source_shape = (count, source, width // HEAD_DIM, HEAD_DIM)
    rows = tokens.reshape(-1, width)
    enc_rows = encoded.reshape(-1, width)
    allowed = visible(target)
    query = (product(rows, self_q) + self_qb).astype(jnp.bfloat16)
    keys = product(rows, self_k).astype(jnp.bfloat16)
    values = (product(rows, self_v) + self_vb).astype(jnp.bfloat16)
    relative = product(rows, bucket_w) + bucket_b
    bias = relative_bias(bucket_table(buckets), relative)
    mixed, logsum = attend(
        query.reshape(head_shape),
        keys.reshape(head_shape),
        values.reshape(head_shape),
        bias,
        allowed,
    )
    mixed = mixed.reshape(rows.shape)
    sum_first = rows + product(mixed, self_o) + self_ob
    first = layer_norm(sum_first, gain_a, shift_a)
    first_low = first.astype(jnp.bfloat16)
    probe = (product(first_low, cross_q) + cross_qb).astype(jnp.bfloat16)
    index = product(enc_rows, cross_k).astype(jnp.bfloat16)
    content = (product(enc_rows, cross_v) + cross_vb).astype(jnp.bfloat16)
    joined, cross_logsum = attend(
        probe.reshape(head_shape),
        index.reshape(source_shape),
        content.reshape(source_shape),
        0.0,
        True,
    )
    joined = joined.reshape(rows.shape)
    sum_second = first + product(joined, cross_o) + cross_ob
    second = layer_norm(sum_second, gain_b, shift_b)
    second_low = second.astype(jnp.bfloat16)
    before = product(second_low, ffn_in) + ffn_inb
    activity = jax.nn.gelu(before, approximate=False).astype(jnp.bfloat16)
    sum_third = second + product(activity, ffn_out) + ffn_outb
    third = layer_norm(sum_third, gain_c, shift_c)
    kept = (
        rows,
        enc_rows,
        query,
        keys,
        values,
        relative,
        logsum,
        mixed,
        sum_first,
        first_low,
        probe,
        index,
        content,
        cross_logsum,
        joined,
        sum_second,
        second_low,
        before,
        activity,
        sum_third,
    )
    return (third, kept)


def backward(whole, kept, cotangent, buckets, lengths):
    (
        self_q,
        self_qb,
        self_k,
        self_v,
        self_vb,
        self_o,
        self_ob,
        bucket_w,
        bucket_b,
        cross_q,
        cross_qb,
        cross_k,
        cross_v,
        cross_vb,
        cross_o,
        cross_ob,
        ffn_in,
        ffn_inb,
        ffn_out,
        ffn_outb,
        gain_a,
        shift_a,
        gain_b,
        shift_b,
        gain_c,
        shift_c,
    ) = whole
    (
        rows,
        enc_rows,
        query,
        keys,
        values,
        relative,
        logsum,
        mixed,
        sum_first,
        first_low,
        probe,
        index,
        content,
        cross_logsum,
        joined,
        sum_second,
        second_low,
        before,
        activity,
        sum_third,
    ) = kept
    count, streams, target, width = cotangent.shape
    source = enc_rows.shape[0] // count
    head_shape = (count, streams * target, width // HEAD_DIM, HEAD_DIM)
    source_shape = (count, source, width // HEAD_DIM, HEAD_DIM)
    allowed = visible(target)
    grad_third = (
        cotangent.reshape(rows.shape).astype(jnp.float32) * valid_rows(lengths, target)[:, None]
    )
    grad_sum_third, grad_gain_c, grad_shift_c = norm_back(sum_third, gain_c, shift_c, grad_third)
    branch_three = grad_sum_third.astype(jnp.bfloat16)
    pair_ffn_out = (activity, branch_three)
    grad_ffn_outb = column_sum(branch_three)
    unused, gelu_pull = jax.vjp(partial(jax.nn.gelu, approximate=False), before)
    grad_before = gelu_pull(product_right(branch_three, ffn_out))[0].astype(jnp.bfloat16)
    pair_ffn_in = (second_low, grad_before)
    grad_ffn_inb = column_sum(grad_before)
    grad_second = grad_sum_third + product_right(grad_before, ffn_in)
    grad_sum_second, grad_gain_b, grad_shift_b = norm_back(sum_second, gain_b, shift_b, grad_second)
    branch_two = grad_sum_second.astype(jnp.bfloat16)
    pair_cross_o = (joined, branch_two)
    grad_cross_ob = column_sum(branch_two)
    grad_joined = product_right(branch_two, cross_o).astype(jnp.bfloat16)
    unused, grad_probe, grad_index, grad_content = attend_back(
        probe.reshape(head_shape),
        index.reshape(source_shape),
        content.reshape(source_shape),
        0.0,
        True,
        cross_logsum,
        grad_joined.reshape(head_shape),
    )
    grad_probe = grad_probe.reshape(rows.shape)
    grad_index = grad_index.reshape(enc_rows.shape)
    grad_content = grad_content.reshape(enc_rows.shape)
    pair_cross_q = (first_low, grad_probe)
    grad_cross_qb = column_sum(grad_probe)
    pair_cross_k = (enc_rows, grad_index)
    pair_cross_v = (enc_rows, grad_content)
    grad_cross_vb = column_sum(grad_content)
    grad_encoded = product_right(grad_index, cross_k) + product_right(grad_content, cross_v)
    grad_first = grad_sum_second + product_right(grad_probe, cross_q)
    grad_sum_first, grad_gain_a, grad_shift_a = norm_back(sum_first, gain_a, shift_a, grad_first)
    branch_one = grad_sum_first.astype(jnp.bfloat16)
    pair_self_o = (mixed, branch_one)
    grad_self_ob = column_sum(branch_one)
    grad_mixed = product_right(branch_one, self_o).astype(jnp.bfloat16)
    onehot = bucket_table(buckets)
    bias = relative_bias(onehot, relative)
    grad_scores, grad_query, grad_keys, grad_values = attend_back(
        query.reshape(head_shape),
        keys.reshape(head_shape),
        values.reshape(head_shape),
        bias,
        allowed,
        logsum,
        grad_mixed.reshape(head_shape),
    )
    grad_relative = jnp.einsum(
        "nqbk,nhqk->nqhb", onehot, grad_scores.astype(jnp.float32), precision=lax.Precision.HIGHEST
    )
    grad_relative = grad_relative.reshape(rows.shape[0], -1).astype(jnp.bfloat16)
    grad_query = grad_query.reshape(rows.shape)
    grad_keys = grad_keys.reshape(rows.shape)
    grad_values = grad_values.reshape(rows.shape)
    pair_self_q = (rows, grad_query)
    grad_self_qb = column_sum(grad_query)
    pair_self_k = (rows, grad_keys)
    pair_self_v = (rows, grad_values)
    grad_self_vb = column_sum(grad_values)
    pair_bucket_w = (rows, grad_relative)
    grad_bucket_b = column_sum(grad_relative)
    grad_tokens = (
        grad_sum_first
        + product_right(grad_query, self_q)
        + product_right(grad_keys, self_k)
        + product_right(grad_values, self_v)
        + product_right(grad_relative, bucket_w)
    )
    pairs = (
        pair_self_q,
        pair_self_k,
        pair_self_v,
        pair_bucket_w,
        pair_self_o,
        pair_cross_k,
        pair_cross_v,
        pair_cross_q,
        pair_cross_o,
        pair_ffn_in,
        pair_ffn_out,
    )
    sums = (
        grad_self_qb,
        grad_self_vb,
        grad_self_ob,
        grad_cross_qb,
        grad_cross_vb,
        grad_cross_ob,
        grad_ffn_outb,
        grad_gain_a,
        grad_shift_a,
        grad_gain_b,
        grad_shift_b,
        grad_gain_c,
        grad_shift_c,
        grad_bucket_b,
        grad_ffn_inb,
    )
    return (
        dict(zip(MATRICES, pairs)),
        dict(zip(NARROW, sums)),
        grad_tokens.reshape(cotangent.shape),
        grad_encoded.reshape(count, source, width),
    )


def per_device(mesh_shape, tokens, encoded, cotangent, buckets, lengths, *shards):
    params = dict(zip(WHOLE, shards))
    dp, fsdp = mesh_shape
    sizes = chips(dp, fsdp)
    valid = valid_rows(lengths, tokens.shape[2])[:, None]
    if any(params[name].shape[0] % ROWS for name in MATRICES):
        whole = tuple(lax.all_gather(params[name], AXES, axis=0, tiled=True) for name in WHOLE)
        third, kept = forward(whole, tokens, encoded, buckets)
        outputs = (third * valid).astype(jnp.bfloat16)
        pairs, sums, grad_tokens, grad_encoded = backward(whole, kept, cotangent, buckets, lengths)
        shares = deliver(pairs, sums)
    else:
        rows = tokens.reshape(-1, tokens.shape[-1])
        enc_rows = encoded.reshape(-1, encoded.shape[-1])
        table = buckets.reshape(rows.shape[0], -1)
        outputs, whole, kept = forward_all(
            sizes,
            spread_small(params),
            [
                quarters(sizes, params[name]) if name == FFN_IN else params[name]
                for name in MATRICES
            ],
            rows,
            enc_rows,
            table,
            valid,
        )
        small, own, grad_tokens, grad_encoded = backward_all(
            sizes, whole, kept, rows, enc_rows, cotangent.reshape(rows.shape), table, valid
        )
        plain = [one for one, name in zip(own, MATRICES) if name != FFN_IN]
        outputs, grad_tokens, grad_encoded, *plain = finish(
            [outputs, grad_tokens, grad_encoded] + plain
        )
        out = dict(zip([name for name in MATRICES if name != FFN_IN], plain))
        grad = own[MATRICES.index(FFN_IN)]
        grad = grad.reshape(GROUP, grad.shape[1], sizes[0] * sizes[1], -1)
        out[FFN_IN] = grad.transpose(1, 2, 0, 3).reshape(params[FFN_IN].shape)
        index = own_index()
        for row, name in enumerate(NARROW):
            width = params[name].shape[0]
            at = lax.rem(index, 128 // width) * width
            out[name] = lax.dynamic_slice(small, (row, at), (1, width)).reshape(width)
        shares = tuple(out[name] for name in WHOLE)
    return (
        outputs.reshape(tokens.shape),
        grad_tokens.reshape(tokens.shape),
        grad_encoded.reshape(encoded.shape),
    ) + shares


def solution(mesh):
    def split(ranks):
        return tuple(P(AXES, *[None] * (rank - 1)) for rank in ranks)

    ranks = tuple(1 if name in NARROW else 2 for name in WHOLE)
    return jax.shard_map(
        partial(per_device, (mesh.shape[AXES[0]], mesh.shape[AXES[1]])),
        mesh=mesh,
        in_specs=split((4, 3, 4, 4, 1) + ranks),
        out_specs=split((4, 4, 3) + ranks),
        check_vma=False,
    )
```

time: 2920 us -> 362 us (0.12)
  waiting for transfers between devices: 2480 us -> 0 us
  Pallas kernels: 0 us -> 347 us
  matrix products: 172 us -> 0 us
  blocking collectives: 108 us -> 0 us
  local copies, waits for them, and re-layouts: 113 us -> 9.06 us
    reduce_scatter x5 -> x0, waiting for transfers between devices: 1140 us -> none  [the longest x1 362 us: backward(): lax.psum_scatter(grad_ffn_out, ('dp', 'fsdp'), scatter_dimension=0, tiled...]
    unnamed x30 -> x0, waiting for transfers between devices: 865 us -> none
    all_gather x11 -> x0, waiting for transfers between devices: 477 us -> none  [the longest x1 75.1 us: per_device(): lax.all_gather(ffn_in, ('dp', 'fsdp'), axis=0, tiled=True)]
    pallas_call x0 -> x3, Pallas kernels: none -> 347 us  [the longest x1 177 us: forward_all(): pl.pallas_call(partial(forward_kernel, sizes, chunks, names), out_shape=[...]
    dot_general x47 -> x0, matrix products: 172 us -> none  [the longest x11 47.5 us: product(): return jnp.dot(left, right, preferred_element_type=jnp.float32)]
    unnamed x155 -> x5, local copies, waits for them, and re-layouts: 82.8 us -> 0.1 us
    all_gather x1 -> x0, blocking collectives: 65.8 us -> none  [per_device(): lax.all_gather(ffn_inb, ('dp', 'fsdp'), axis=0, tiled=True)]
    unnamed x1 -> x0, blocking collectives: 42.5 us -> none
  transfers between devices with their start and end apart: 23 -> 0, of which waited for: 21 -> 0; matrix products, arithmetic and copies ran while one was open for 7% -> 0% of each run, Pallas kernels for 0% -> 0%
where the time goes in v1:
time: 362 us; the launch traced here: 359 us
  Pallas kernels  347 us (96%)
  local copies, waits for them, and re-layouts  9.06 us (3%)
    pallas_call x1, Pallas kernels, forward_all(): pl.pallas_call(partial(forward_kernel, sizes, chunks, names), out_shape=[...  177 us
    pallas_call x1, Pallas kernels, backward_all(): pl.pallas_call(partial(backward_kernel, sizes, chunks, flat_room), out_sh...  165 us

profile of v1, /device:TPU:0, one launch (start us, length us, event | category | flops | bytes accessed | tf_op | source)
XLA Modules:
  0.0 359.1 jit_solution(9517414314519209417)
XLA Ops:
  1.4 0.7 fusion.2
  2.0 0.7 tile.19
  2.7 0.1 tile.20
  2.8 1.5 stack.56
  4.3 0.1 tile.18
  4.5 0.6 pad_maximum_fusion.refs_4_
  5.1 0.8 copy.63.refs_3_.refs_2_
  5.9 1.1 reshape.297
  7.0 0.8 reshape.298.refs_14_
  7.8 176.9 %forward_all.1 = (bf16[256,1024]{1,0:T(8,128)(2,1)}, bf16[1,4,2,2,2,32,1024]{6,5,4,3,2,1,0:T(8,128)(2,1)}, bf16[1,4,2,2,2,32,1024]{6,5,4,3,2,1,0:T(8,128)(2,1)},...) custom-call(bf16[256,1024]{1,0:T(8,128)(2,1)} %bitcast.89, ...), custom_call_target="tpu_custom_call" | custom-call | flops 10000000000 | bytes 134217728 | tf_op jit(solution)/shard_map/forward_all/pallas_call | solution.py:621
  184.8 165.2 %backward_all.1 = (f32[16,128]{1,0:T(8,128)}, f32[32,1024]{1,0:T(8,128)}, f32[32,1024]{1,0:T(8,128)}, f32[32,1024]{1,0:T(8,128)}, f32[32,512]{1,0:T(8,128)}, /*i...) custom-call(bf16[256,1024]{1,0:T(8,128)(2,1)} %bitcast.91, ...), custom_call_target="tpu_custom_call" | custom-call | flops 20000000000 | bytes 134217728 | tf_op jit(solution)/shard_map/backward_all/pallas_call | solution.py:1422
  350.0 1.3 dynamic-slice_bitcast_fusion.10
  351.3 0.0 copy-start.1
  351.3 0.0 copy-start
  351.3 5.0 %finish.1 = (bf16[256,1024]{1,0:T(8,128)(2,1)}, f32[256,1024]{1,0:T(8,128)}, f32[512,1024]{1,0:T(8,128)}, f32[32,1024]{1,0:T(8,128)}, f32[32,1024]{1,0:T(8,128)}...) custom-call(bf16[256,1024]{1,0:T(8,128)(2,1)} %get-tuple-element.86., ...), custom_call_target="tpu_custom_call" | custom-call | tf_op jit(solution)/shard_map/finish/pallas_call | solution.py:1492
  356.3 0.0 copy-done.1
  356.3 0.5 slice_bitcast_fusion
  356.8 0.6 dynamic-slice_bitcast_fusion
  357.4 0.0 copy-done
  357.4 0.1 copy.66
  357.6 0.3 copy.65
  357.9 1.0 reshape.311
  (9 shorter events, 0.1 us)
Async XLA Ops:
  351.3 5.0 %copy-start.1 = (f32[16,128]{1,0:T(8,128)S(1)}, f32[16,128]{1,0:T(8,128)}, u32[]{:S(2)}) copy-start(f32[16,128]{1,0:T(8,128)} %get-tuple-element.132) | copy-start | bytes 24580
  351.3 6.2 %copy-start = (f32[4,32,1024]{2,1,0:T(8,128)S(1)}, f32[4,32,1024]{2,1,0:T(8,128)}, u32[]{:S(2)}) copy-start(f32[4,32,1024]{2,1,0:T(8,128)} %get-tuple-element.141) | copy-start | bytes 1572868

commit v2 on v1

--- a/solution.py
+++ b/solution.py
@@ -15,6 +15,7 @@
 AHEAD = 3
 LINES = 64
 LAG = 2
+GATHER_LAG = 1
 AXES = ("dp", "fsdp")
 (
     SELF_Q, SELF_K, SELF_V, BUCKET_W, SELF_O, CROSS_K,
@@ -53,7 +54,7 @@
 PARTIALS, PARTIAL_OTHER, PARTIAL_DIAGONAL, PARTIAL_NEXT = 25, 29, 30, 31
 GATHER_ORDER = (
     SELF_Q, SELF_K, SELF_V, BUCKET_W, SELF_O, CROSS_Q, CROSS_K, CROSS_V,
-    FFN_IN, FFN_IN, CROSS_O, FFN_IN, FFN_IN, FFN_OUT, FFN_OUT, FFN_OUT, FFN_OUT,
+    CROSS_O, FFN_IN, FFN_IN, FFN_IN, FFN_IN, FFN_OUT, FFN_OUT, FFN_OUT, FFN_OUT,
 )
 GROUP = 4
 NEXT, OTHER, DIAGONAL = 1, 2, 3
@@ -279,7 +280,7 @@
         if now + AHEAD < total:
             start(now + AHEAD, 0)
         for stage in range(4):
-            number = now - LAG * stage
+            number = now - GATHER_LAG * stage
             if 0 <= number < total:
                 pass_on(number, stage)
 
@@ -522,24 +523,23 @@
             norm(held[SUM_SECOND], GAIN_B, SHIFT_B, second, lows.at[0])
             share(NEXT).start()
             share(OTHER).start()
-            feed(number - 2, 0)
-            feed(number - 1, 0)
-        elif name == FFN_IN and part >= 2:
+        elif name == FFN_IN:
             feed(number, 0)
             if part == 2:
                 share(OTHER).wait_recv()
-                for earlier in (number - 3, number - 2):
+                for earlier in (number - 2, number - 1):
                     feed(earlier, OTHER)
                 share(NEXT).wait_recv()
                 share(DIAGONAL).start()
-                for earlier in (number - 3, number - 2):
+                for earlier in (number - 2, number - 1):
                     feed(earlier, NEXT)
                 share(DIAGONAL).wait_recv()
-                for earlier in (number - 3, number - 2):
+                for earlier in (number - 2, number - 1):
                     feed(earlier, DIAGONAL)
                 save(SECOND_LOW)
-            for item in (OTHER, NEXT, DIAGONAL):
-                feed(number, item)
+            if part >= 2:
+                for item in (OTHER, NEXT, DIAGONAL):
+                    feed(number, item)
             if part == 3:
                 save(SLOPE, ACTIVITY)
         elif name == FFN_OUT:
@@ -552,10 +552,14 @@
     enter(sizes, me)
     for number in range(min(AHEAD, total)):
         start(number, 0)
-    for now in range(total + 3 * LAG):
+    done = 0
+    for now in range(total + 3 * GATHER_LAG):
         turn(now)
-        if now >= 3 * LAG:
-            compute(now - 3 * LAG)
+        while done < total and (
+            done + GATHER_LAG * (len(gather_route(chunks[done][0], 0)) - 1) <= now
+        ):
+            compute(done)
+            done += 1
     relay(GROUP - 1)
     wide = width // GROUP
     for part in range(GROUP):

time: 362 us -> 356 us (0.983)
  Pallas kernels: 347 us -> 340 us
    pallas_call x1, Pallas kernels: 177 us -> 164 us  [forward_all(): pl.pallas_call(partial(forward_kernel, sizes, chunks, names), out_shape=[...]
    pallas_call x1, Pallas kernels: 165 us -> 172 us  [backward_all(): pl.pallas_call(partial(backward_kernel, sizes, chunks, flat_room), out_sh...]
where the time goes in v2:
time: 356 us; the launch traced here: 352 us
  Pallas kernels  340 us (96%)
  local copies, waits for them, and re-layouts  9.06 us (3%)
    pallas_call x1, Pallas kernels, backward_all(): pl.pallas_call(partial(backward_kernel, sizes, chunks, flat_room), out_sh...  172 us
    pallas_call x1, Pallas kernels, forward_all(): pl.pallas_call(partial(forward_kernel, sizes, chunks, names), out_shape=[...  164 us

profile of v2, /device:TPU:0, one launch (start us, length us, event | category | flops | bytes accessed | tf_op | source)
XLA Modules:
  0.0 352.5 jit_solution(17265129979476457136)
XLA Ops:
  1.4 0.7 fusion.2
  2.0 0.7 tile.19
  2.7 0.1 tile.20
  2.8 1.5 stack.56
  4.3 0.1 tile.18
  4.5 0.6 pad_maximum_fusion.refs_4_
  5.1 0.8 copy.63.refs_3_.refs_2_
  5.9 1.1 reshape.297
  7.0 0.8 reshape.298.refs_14_
  7.8 163.8 %forward_all.1 = (bf16[256,1024]{1,0:T(8,128)(2,1)}, bf16[1,4,2,2,2,32,1024]{6,5,4,3,2,1,0:T(8,128)(2,1)}, bf16[1,4,2,2,2,32,1024]{6,5,4,3,2,1,0:T(8,128)(2,1)},...) custom-call(bf16[256,1024]{1,0:T(8,128)(2,1)} %bitcast.89, ...), custom_call_target="tpu_custom_call" | custom-call | flops 10000000000 | bytes 134217728 | tf_op jit(solution)/shard_map/forward_all/pallas_call | solution.py:625
  171.6 171.7 %backward_all.1 = (f32[16,128]{1,0:T(8,128)}, f32[32,1024]{1,0:T(8,128)}, f32[32,1024]{1,0:T(8,128)}, f32[32,1024]{1,0:T(8,128)}, f32[32,512]{1,0:T(8,128)}, /*i...) custom-call(bf16[256,1024]{1,0:T(8,128)(2,1)} %bitcast.91, ...), custom_call_target="tpu_custom_call" | custom-call | flops 20000000000 | bytes 134217728 | tf_op jit(solution)/shard_map/backward_all/pallas_call | solution.py:1426
  343.3 1.3 dynamic-slice_bitcast_fusion.10
  344.6 0.0 copy-start.1
  344.6 0.0 copy-start
  344.6 5.0 %finish.1 = (bf16[256,1024]{1,0:T(8,128)(2,1)}, f32[256,1024]{1,0:T(8,128)}, f32[512,1024]{1,0:T(8,128)}, f32[32,1024]{1,0:T(8,128)}, f32[32,1024]{1,0:T(8,128)}...) custom-call(bf16[256,1024]{1,0:T(8,128)(2,1)} %get-tuple-element.86., ...), custom_call_target="tpu_custom_call" | custom-call | tf_op jit(solution)/shard_map/finish/pallas_call | solution.py:1496
  349.6 0.0 copy-done.1
  349.6 0.5 slice_bitcast_fusion
  350.1 0.6 dynamic-slice_bitcast_fusion
  350.8 0.0 copy-done
  350.8 0.1 copy.66
  350.9 0.3 copy.65
  351.3 1.0 reshape.311
  (9 shorter events, 0.1 us)
Async XLA Ops:
  344.6 5.0 %copy-start.1 = (f32[16,128]{1,0:T(8,128)S(1)}, f32[16,128]{1,0:T(8,128)}, u32[]{:S(2)}) copy-start(f32[16,128]{1,0:T(8,128)} %get-tuple-element.132) | copy-start | bytes 24580
  344.6 6.2 %copy-start = (f32[4,32,1024]{2,1,0:T(8,128)S(1)}, f32[4,32,1024]{2,1,0:T(8,128)}, u32[]{:S(2)}) copy-start(f32[4,32,1024]{2,1,0:T(8,128)} %get-tuple-element.141) | copy-start | bytes 1572868
